TPU v7x, 32 devices: a whole 2x2x4 slice. The times are simulated.
32 devices in a mesh: dp: 8 (over z, x), layer: 4 (over y, core).
Axes of the slice: x: 2, y: 2, z: 4, core: 2. Of those that a mesh axis runs over, the one named last changes fastest.
Arguments:
- audio_in: float32 [8, 49152], P(None, 'dp'), may hold values from -6 to 6
- mel_spec: bfloat16 [80, 49152], P(None, 'dp'), may hold values from -6 to 6
- lengths: int32 [32, 4], P('dp'), may hold values from 1 to 1024, 1536 in all within a row
- z_cotangent: float32 [8, 49152], P(None, 'dp'), may hold values from -6 to 6
- det_cotangent: float32 [49152], P('dp'), may hold values from -6 to 6
- lu_weight: float32 [8, 8], replicated, may hold values from -1.2 to 1.2
- start_weight: float32 [512, 4], replicated, may hold values from -3 to 3
- start_bias: float32 [512], replicated, may hold values from -3 to 3
- in_weight: bfloat16 [4, 1024, 1536], P('layer'), may hold values from -0.15625 to 0.15625
- cond_weight: bfloat16 [4, 1024, 80], P('layer'), may hold values from -0.625 to 0.625
- gate_bias: float32 [4, 1024], P('layer'), may hold values from -3 to 3
- mix_weight: bfloat16 [4, 768, 512], P('layer'), may hold values from -0.25 to 0.25
- mix_bias: float32 [4, 768], P('layer'), may hold values from -2 to 2
- end_weight: bfloat16 [8, 768], replicated, may hold values from -0.109375 to 0.109375
- end_bias: float32 [8], replicated, may hold values from -1.5 to 1.5
Outputs:
- latent: float32 [8, 49152], P(None, ('dp', 'layer'))
- logdet: float32 [49152], P(('dp', 'layer'))
- audio_grad: float32 [8, 49152], P(None, ('dp', 'layer'))
- mel_grad: float32 [80, 49152], P(None, ('dp', 'layer'))
- lu_grad: float32 [8, 8], replicated
- start_weight_grad: float32 [512, 4], replicated
- start_bias_grad: float32 [512], replicated
- in_weight_grad: float32 [4, 1024, 1536], P('layer', 'dp')
- cond_weight_grad: float32 [4, 1024, 80], P('layer', 'dp')
- gate_bias_grad: float32 [4, 1024], P('layer', 'dp')
- mix_weight_grad: float32 [4, 768, 512], P('layer', 'dp')
- mix_bias_grad: float32 [4, 768], P('layer', 'dp')
- end_weight_grad: float32 [8, 768], replicated
- end_bias_grad: float32 [8], replicated
Inputs may be any that keep to these rules, and one draw needn't show every extreme that they name: `lengths`: each row sums to 1536 exactly and its largest entry is 1024.
All inputs are finite; a program needn't handle non-finite values.
Results may differ from a plain program's by a relative error of at most 0.023.
Values may be sent and summed in bfloat16 or wider, within the bound.
No kernel may reach another device: no remote copies, remote signals or barrier semaphores. Data moves between devices by JAX's collectives and lax.ppermute only.
A program may use at most 320 MiB of HBM per device.

v0:
```python
import jax
import jax.numpy as jnp
from jax import lax
from jax.sharding import PartitionSpec as P

highest = lax.Precision.HIGHEST


def shifted(block, axis, distance):
    devices = range(lax.axis_size(axis))
    route = [(i - distance, i) for i in devices if i - distance in devices]
    return lax.ppermute(block, axis, route)


def flow_matrix(lu_weight):
    size_now = lu_weight.shape[0]
    lower = jnp.tril(lu_weight, -1) + jnp.eye(size_now, dtype=lu_weight.dtype)
    upper = jnp.triu(lu_weight, 1) + jnp.diag(jnp.exp(jnp.diagonal(lu_weight)))
    return jnp.dot(lower, upper, precision=highest)


def rooms(lengths, row_count):
    ends = jnp.cumsum(lengths, axis=1)
    starts = ends - lengths
    places = jnp.arange(row_count, dtype=jnp.int32)[None, None, :]
    inside = (places >= starts[:, :, None]) & (places < ends[:, :, None])
    left_room = jnp.sum(jnp.where(inside, places - starts[:, :, None], 0), axis=1)
    right_room = jnp.sum(jnp.where(inside, ends[:, :, None] - 1 - places, 0), axis=1)
    return (left_room, right_room)


def move_rows(values, offset, margin):
    row_count = values.shape[1]
    padded = jnp.pad(values, ((0, 0), (margin, margin)))
    return lax.dynamic_slice_in_dim(padded, margin + offset, row_count, 1)


def spread_taps(stream, dilation, margin, keep_before, keep_after):
    before = move_rows(stream, -dilation, margin) * keep_before
    after = move_rows(stream, dilation, margin) * keep_after
    return jnp.concatenate([before, stream, after], axis=0)


def contract(first, second, first_dim, second_dim):
    return lax.dot_general(
        first, second, (((first_dim,), (second_dim,)), ((), ())), preferred_element_type=jnp.float32
    )


def pick(stack, micro_slot, axis_number):
    return lax.dynamic_index_in_dim(stack, micro_slot, axis_number, keepdims=False)


def place_in(stack, piece, micro_slot, flag, axis_number):
    old_piece = pick(stack, micro_slot, axis_number)
    return lax.dynamic_update_index_in_dim(
        stack, jnp.where(flag, piece, old_piece), micro_slot, axis_number
    )


def per_device(
    audio_in,
    mel_spec,
    lengths,
    z_cotangent,
    det_cotangent,
    lu_weight,
    start_weight,
    start_bias,
    in_weight,
    cond_weight,
    gate_bias,
    mix_weight,
    mix_bias,
    end_weight,
    end_bias,
):
    cycle_size = lax.axis_size("layer")
    layer_place = lax.axis_index("layer")
    margin = 2 ** (cycle_size - 1)
    dilation = jnp.left_shift(jnp.int32(1), layer_place)
    micro_count = lengths.shape[0]
    row_count = audio_in.shape[1] // micro_count
    group_size = audio_in.shape[0]
    half = group_size // 2
    res_width = start_weight.shape[0]
    mel_width = mel_spec.shape[0]
    layer_in = in_weight[0]
    layer_cond = cond_weight[0]
    layer_gate_bias = gate_bias[0]
    layer_mix = mix_weight[0]
    layer_mix_bias = mix_bias[0]
    gate_width = layer_in.shape[0]
    skip_width = layer_mix.shape[0] - res_width
    is_first = layer_place == 0
    is_last = layer_place == cycle_size - 1
    first_flag = is_first.astype(jnp.float32)
    last_flag = is_last.astype(jnp.float32)
    steps_total = micro_count + cycle_size - 1
    left_room, right_room = rooms(lengths, row_count)
    keep_before_all = (left_room >= dilation).astype(jnp.bfloat16)
    keep_after_all = (right_room >= dilation).astype(jnp.bfloat16)
    matrix = flow_matrix(lu_weight)
    mixed = jnp.dot(matrix, audio_in, precision=highest).reshape(group_size, micro_count, row_count)
    front = mixed[:half]
    back = mixed[half:]
    start_blocks = (
        jnp.einsum("rc,cmt->mrt", start_weight, front, precision=highest)
        + start_bias[None, :, None]
    ).astype(jnp.bfloat16)
    mel_blocks = mel_spec.reshape(mel_width, micro_count, row_count)

    def taps_of(stream, micro_slot):
        keep_before = pick(keep_before_all, micro_slot, 0)[None, :]
        keep_after = pick(keep_after_all, micro_slot, 0)[None, :]
        stacked = spread_taps(stream, dilation, margin, keep_before, keep_after)
        return (stacked, keep_before, keep_after)

    def ahead_step(step_number, carry):
        recv_stream, recv_skip, kept_stream, kept_gate, final_stream, skip_store = carry
        micro_index = step_number - layer_place
        is_valid = (micro_index >= 0) & (micro_index < micro_count)
        micro_slot = jnp.clip(micro_index, 0, micro_count - 1)
        stream_in = jnp.where(is_first, pick(start_blocks, micro_slot, 0), recv_stream)

        def ahead_work(unused):
            stacked, keep_before, keep_after = taps_of(stream_in, micro_slot)
            mel_block = pick(mel_blocks, micro_slot, 1)
            pre_gate = jnp.dot(layer_in, stacked, preferred_element_type=jnp.float32)
            pre_gate = (
                pre_gate
                + jnp.dot(layer_cond, mel_block, preferred_element_type=jnp.float32)
                + layer_gate_bias[:, None]
            )
            gated = (jnp.tanh(pre_gate[:res_width]) * jax.nn.sigmoid(pre_gate[res_width:])).astype(
                jnp.bfloat16
            )
            branch = (
                jnp.dot(layer_mix, gated, preferred_element_type=jnp.float32)
                + layer_mix_bias[:, None]
            )
            return (pre_gate, branch)

        def ahead_rest(unused):
            return (
                jnp.zeros((gate_width, row_count), jnp.float32),
                jnp.zeros((res_width + skip_width, row_count), jnp.float32),
            )

        pre_gate, branch = lax.cond(is_valid, ahead_work, ahead_rest, 0)
        stream_out = (stream_in.astype(jnp.float32) + branch[:res_width]).astype(jnp.bfloat16)
        kept_stream = place_in(kept_stream, stream_in, micro_slot, is_valid, 0)
        kept_gate = place_in(kept_gate, pre_gate, micro_slot, is_valid, 0)
        final_stream = place_in(final_stream, stream_out, micro_slot, is_valid & is_last, 0)
        skip_out = jnp.where(is_first, jnp.zeros_like(recv_skip), recv_skip) + branch[res_width:]
        skip_store = place_in(skip_store, skip_out, micro_slot, is_valid & is_last, 0)
        recv_skip = shifted(skip_out, "layer", 1)
        recv_stream = shifted(stream_out, "layer", 1)
        return (recv_stream, recv_skip, kept_stream, kept_gate, final_stream, skip_store)

    ahead_init = (
        jnp.zeros((res_width, row_count), jnp.bfloat16),
        jnp.zeros((skip_width, row_count), jnp.float32),
        jnp.zeros((micro_count, res_width, row_count), jnp.bfloat16),
        jnp.zeros((micro_count, gate_width, row_count), jnp.float32),
        jnp.zeros((micro_count, res_width, row_count), jnp.bfloat16),
        jnp.zeros((micro_count, skip_width, row_count), jnp.float32),
    )
    ahead_final = lax.fori_loop(0, steps_total, ahead_step, ahead_init)
    kept_stream = ahead_final[2]
    kept_gate = ahead_final[3]
    final_stream = ahead_final[4]
    skip_store = ahead_final[5]
    end_in = jnp.concatenate([final_stream, skip_store.astype(jnp.bfloat16)], axis=1)
    result = (
        jnp.einsum("oc,mct->omt", end_weight, end_in, preferred_element_type=jnp.float32)
        + end_bias[:, None, None]
    )
    log_scale = result[:half]
    shift_part = result[half:]
    growth = jnp.exp(log_scale)
    coupled = growth * back + shift_part
    latent_full = jnp.concatenate([front, coupled], axis=0).reshape(group_size, -1)
    logdet_full = (jnp.sum(log_scale, axis=0) + jnp.trace(lu_weight)).reshape(-1)
    z_grad_in = z_cotangent.reshape(group_size, micro_count, row_count)
    det_grad_in = det_cotangent.reshape(micro_count, row_count)
    coupled_grad = z_grad_in[half:]
    result_grad = jnp.concatenate(
        [coupled_grad * growth * back + det_grad_in[None], coupled_grad], axis=0
    ).astype(jnp.bfloat16)
    back_grad = coupled_grad * growth
    end_weight_grad = (
        jnp.einsum("omt,mct->oc", result_grad, end_in, preferred_element_type=jnp.float32)
        * last_flag
    )
    end_bias_grad = jnp.sum(result_grad.astype(jnp.float32), axis=(1, 2)) * last_flag
    end_in_grad = jnp.einsum(
        "oc,omt->mct", end_weight, result_grad, preferred_element_type=jnp.float32
    )
    final_grad = end_in_grad[:, :res_width].astype(jnp.bfloat16)
    skip_grad = end_in_grad[:, res_width:].astype(jnp.bfloat16)
    totals_init = (
        jnp.zeros(layer_in.shape, jnp.float32),
        jnp.zeros(layer_cond.shape, jnp.float32),
        jnp.zeros((gate_width,), jnp.float32),
        jnp.zeros(layer_mix.shape, jnp.float32),
        jnp.zeros((res_width + skip_width,), jnp.float32),
    )

    def back_step(step_number, carry):
        recv_grad, recv_skip_grad, first_grads, mel_grads, totals = carry
        micro_index = step_number - (cycle_size - 1 - layer_place)
        is_valid = (micro_index >= 0) & (micro_index < micro_count)
        micro_slot = jnp.clip(micro_index, 0, micro_count - 1)
        grad_out = jnp.where(is_last, pick(final_grad, micro_slot, 0), recv_grad)
        grad_skip = jnp.where(is_last, pick(skip_grad, micro_slot, 0), recv_skip_grad)

        def back_work(unused):
            pre_gate = pick(kept_gate, micro_slot, 0)
            stream_in = pick(kept_stream, micro_slot, 0)
            stacked, keep_before, keep_after = taps_of(stream_in, micro_slot)
            mel_block = pick(mel_blocks, micro_slot, 1)
            tanh_part = jnp.tanh(pre_gate[:res_width])
            sig_part = jax.nn.sigmoid(pre_gate[res_width:])
            gated = (tanh_part * sig_part).astype(jnp.bfloat16)
            branch_grad = jnp.concatenate([grad_out, grad_skip], axis=0)
            mix_grad = contract(branch_grad, gated, 1, 1)
            mix_bias_grad = jnp.sum(branch_grad.astype(jnp.float32), axis=1)
            gated_grad = contract(layer_mix, branch_grad, 0, 0)
            pre_grad = jnp.concatenate(
                [
                    gated_grad * sig_part * (1.0 - tanh_part * tanh_part),
                    gated_grad * tanh_part * sig_part * (1.0 - sig_part),
                ],
                axis=0,
            ).astype(jnp.bfloat16)
            in_grad = contract(pre_grad, stacked, 1, 1)
            cond_grad = contract(pre_grad, mel_block, 1, 1)
            gate_bias_grad = jnp.sum(pre_grad.astype(jnp.float32), axis=1)
            stacked_grad = contract(layer_in, pre_grad, 0, 0)
            mel_part_grad = contract(layer_cond, pre_grad, 0, 0)
            stream_grad = stacked_grad[res_width : 2 * res_width]
            stream_grad = stream_grad + move_rows(
                stacked_grad[:res_width] * keep_before, dilation, margin
            )
            stream_grad = stream_grad + move_rows(
                stacked_grad[2 * res_width :] * keep_after, -dilation, margin
            )
            grad_in = (grad_out.astype(jnp.float32) + stream_grad).astype(jnp.bfloat16)
            step_grads = (in_grad, cond_grad, gate_bias_grad, mix_grad, mix_bias_grad)
            return (step_grads, mel_part_grad, grad_in)

        def back_rest(unused):
            zero_grads = tuple(jax.tree.map(jnp.zeros_like, totals_init))
            return (
                zero_grads,
                jnp.zeros((mel_width, row_count), jnp.float32),
                jnp.zeros((res_width, row_count), jnp.bfloat16),
            )

        step_grads, mel_part_grad, grad_in = lax.cond(is_valid, back_work, back_rest, 0)
        mel_grads = place_in(mel_grads, mel_part_grad, micro_slot, is_valid, 1)
        first_grads = place_in(first_grads, grad_in, micro_slot, is_valid & is_first, 0)
        totals = jax.tree.map(lambda running, addend: running + addend, totals, tuple(step_grads))
        recv_grad = shifted(grad_in, "layer", -1)
        recv_skip_grad = shifted(grad_skip, "layer", -1)
        return (recv_grad, recv_skip_grad, first_grads, mel_grads, totals)

    back_init = (
        jnp.zeros((res_width, row_count), jnp.bfloat16),
        jnp.zeros((skip_width, row_count), jnp.bfloat16),
        jnp.zeros((micro_count, res_width, row_count), jnp.bfloat16),
        jnp.zeros((mel_width, micro_count, row_count), jnp.float32),
        totals_init,
    )
    back_final = lax.fori_loop(0, steps_total, back_step, back_init)
    first_grads = back_final[2]
    mel_grads = back_final[3]
    totals = back_final[4]
    shares = (
        lax.psum_scatter(
            totals[0].astype(jnp.bfloat16), "dp", scatter_dimension=0, tiled=True
        ).astype(jnp.float32),
        lax.psum_scatter(
            totals[1].astype(jnp.bfloat16), "dp", scatter_dimension=0, tiled=True
        ).astype(jnp.float32),
        lax.psum_scatter(
            totals[2].astype(jnp.bfloat16), "dp", scatter_dimension=0, tiled=True
        ).astype(jnp.float32),
        lax.psum_scatter(
            totals[3].astype(jnp.bfloat16), "dp", scatter_dimension=0, tiled=True
        ).astype(jnp.float32),
        lax.psum_scatter(
            totals[4].astype(jnp.bfloat16), "dp", scatter_dimension=0, tiled=True
        ).astype(jnp.float32),
    )
    first_float = first_grads.astype(jnp.float32)
    start_weight_grad = (
        jnp.einsum("mrt,cmt->rc", first_float, front, precision=highest) * first_flag
    )
    start_bias_grad = jnp.sum(first_float, axis=(0, 2)) * first_flag
    front_grad = (
        jnp.einsum("rc,mrt->cmt", start_weight, first_float, precision=highest) * first_flag
        + z_grad_in[:half] * last_flag
    )
    mixed_grad = jnp.concatenate([front_grad, back_grad * last_flag], axis=0).reshape(
        group_size, -1
    )
    frame_stack = jnp.concatenate(
        [
            latent_full * last_flag,
            logdet_full[None, :] * last_flag,
            mixed_grad,
            mel_grads.reshape(mel_width, -1),
        ],
        axis=0,
    )
    frame_share = lax.psum_scatter(
        frame_stack.astype(jnp.bfloat16), "layer", scatter_dimension=1, tiled=True
    ).astype(jnp.float32)
    latent = frame_share[:group_size]
    logdet = frame_share[group_size]
    mixed_share = frame_share[group_size + 1 : 2 * group_size + 1]
    mel_share = frame_share[2 * group_size + 1 :]
    share_cols = frame_share.shape[1]
    audio_local = lax.dynamic_slice_in_dim(audio_in, layer_place * share_cols, share_cols, 1)
    audio_share = jnp.dot(matrix.T, mixed_share, precision=highest)
    matrix_grad = jnp.dot(mixed_share, audio_local.T, precision=highest)
    unused_values, pullback = jax.vjp(
        lambda params: (flow_matrix(params), jnp.trace(params)), lu_weight
    )
    (lu_grad,) = pullback((matrix_grad, jnp.sum(det_cotangent) * last_flag))
    lu_grad, start_weight_grad, start_bias_grad, end_weight_grad, end_bias_grad = lax.psum(
        (lu_grad, start_weight_grad, start_bias_grad, end_weight_grad, end_bias_grad),
        ("dp", "layer"),
    )
    return (
        latent,
        logdet,
        audio_share,
        mel_share,
        lu_grad,
        start_weight_grad,
        start_bias_grad,
        shares[0][None],
        shares[1][None],
        shares[2][None],
        shares[3][None],
        shares[4][None],
        end_weight_grad,
        end_bias_grad,
    )


def solution(mesh):
    in_specs = (
        P(None, "dp"),
        P(None, "dp"),
        P("dp", None),
        P(None, "dp"),
        P("dp"),
        P(),
        P(),
        P(),
        P("layer", None, None),
        P("layer", None, None),
        P("layer", None),
        P("layer", None, None),
        P("layer", None),
        P(),
        P(),
    )
    out_specs = (
        P(None, ("dp", "layer")),
        P(("dp", "layer")),
        P(None, ("dp", "layer")),
        P(None, ("dp", "layer")),
        P(),
        P(),
        P(),
        P("layer", "dp", None),
        P("layer", "dp", None),
        P("layer", "dp"),
        P("layer", "dp", None),
        P("layer", "dp"),
        P(),
        P(),
    )
    return jax.shard_map(
        per_device, mesh=mesh, in_specs=in_specs, out_specs=out_specs, check_vma=False
    )
```

profile of v0, /device:TPU:0, one launch (start us, length us, event | category | flops | bytes accessed | tf_op | source)
XLA Modules:
  0.0 1366.5 jit_solution(10400722001975479404)
XLA Ops:
  19.2 12.0 fusion.49
  31.2 11.5 broadcast_in_dim.179.clone
  53.5 569.3 %while.55 = (s32[]{:T(128)}, bf16[512,1536]{0,1:T(8,128)(2,1)}, f32[256,1536]{0,1:T(8,128)}, bf16[4,512,1536]{2,1,0:T(8,128)(2,1)}, f32[4,1024,1536]{2,1,0:T(8,1...) while((s32[]{:T(128)}, bf16[512,1536]{0,1:T(8,128)(2,1)}, ...), condition=%wide.region_6.7_spmd, body=%wide.region_3.6_spmd.sunk | while | flops 6327631872 | bytes 228377904 | solution.py:169
  62.5 22.8 %conditional.5 = (f32[1024,1536]{0,1:T(8,128)}, f32[768,1536]{0,1:T(8,128)}) conditional(s32[]{:T(128)} %convert_element_type.176, () %tuple.144, (bf16[512,1536]{0,1:T(8,128)(2,1)S(1)}, s32[]{:T(128)}, s32[]{:T(128)}, bf16[4,1536]{1,0:T(4,128)(2,1)S(1)}, bf16[4,1536]{1,0:T(4,128)(2,1)S(1)}, /*index=5*/bf16[1024,1536]{1,0:T(8,128)(2,1)}, ...), branch_computations={%region_4.4_spmd, %region_5.5_spmd} | conditional | flops 6320160768 | bytes 66370812 | solution.py:150
  111.4 9.4 fusion.118
  150.4 22.8 %conditional.5 = (f32[1024,1536]{0,1:T(8,128)}, f32[768,1536]{0,1:T(8,128)}) conditional(s32[]{:T(128)} %convert_element_type.176, () %tuple.144, (bf16[512,1536]{0,1:T(8,128)(2,1)S(1)}, s32[]{:T(128)}, s32[]{:T(128)}, bf16[4,1536]{1,0:T(4,128)(2,1)S(1)}, bf16[4,1536]{1,0:T(4,128)(2,1)S(1)}, /*index=5*/bf16[1024,1536]{1,0:T(8,128)(2,1)}, ...), branch_computations={%region_4.4_spmd, %region_5.5_spmd} | conditional | flops 6320160768 | bytes 66370812 | solution.py:150
  199.3 9.4 fusion.118
  238.2 22.8 %conditional.5 = (f32[1024,1536]{0,1:T(8,128)}, f32[768,1536]{0,1:T(8,128)}) conditional(s32[]{:T(128)} %convert_element_type.176, () %tuple.144, (bf16[512,1536]{0,1:T(8,128)(2,1)S(1)}, s32[]{:T(128)}, s32[]{:T(128)}, bf16[4,1536]{1,0:T(4,128)(2,1)S(1)}, bf16[4,1536]{1,0:T(4,128)(2,1)S(1)}, /*index=5*/bf16[1024,1536]{1,0:T(8,128)(2,1)}, ...), branch_computations={%region_4.4_spmd, %region_5.5_spmd} | conditional | flops 6320160768 | bytes 66370812 | solution.py:150
  287.1 9.4 fusion.118
  326.0 22.8 %conditional.5 = (f32[1024,1536]{0,1:T(8,128)}, f32[768,1536]{0,1:T(8,128)}) conditional(s32[]{:T(128)} %convert_element_type.176, () %tuple.144, (bf16[512,1536]{0,1:T(8,128)(2,1)S(1)}, s32[]{:T(128)}, s32[]{:T(128)}, bf16[4,1536]{1,0:T(4,128)(2,1)S(1)}, bf16[4,1536]{1,0:T(4,128)(2,1)S(1)}, /*index=5*/bf16[1024,1536]{1,0:T(8,128)(2,1)}, ...), branch_computations={%region_4.4_spmd, %region_5.5_spmd} | conditional | flops 6320160768 | bytes 66370812 | solution.py:150
  374.9 9.4 fusion.118
  644.0 477.3 %while.56 = (s32[]{:T(128)}, bf16[512,1536]{0,1:T(8,128)(2,1)}, bf16[256,1536]{0,1:T(8,128)(2,1)}, bf16[4,512,1536]{1,2,0:T(8,128)(2,1)}, bf16[80,4,1536]{2,0,1:...) while((s32[]{:T(128)}, bf16[512,1536]{0,1:T(8,128)(2,1)}, ...), condition=%wide.region_14.15_spmd.clone, body=%wide.region_9.14_spmd.clone.sunk | while | flops 12677576704 | bytes 228522000 | solution.py:276
  683.5 8.7 select_add_fusion.13
  726.8 51.4 %collective-permute-done.3 = bf16[256,1536]{0,1:T(8,128)(2,1)} collective-permute-done((bf16[256,1536]{0,1:T(8,128)(2,1)}, bf16[256,1536]{0,1:T(8,128)(2,1)}, u32[]{:S(2)}, u32[]{:S(2)}) %collective-permute-start.3) | collective-permute-done | bytes 786464 | tf_op jit(solution)/shard_map/while/body/eval_jaxpr/ppermute | solution.py:12
  778.2 50.4 %collective-permute-done.2 = bf16[512,1536]{0,1:T(8,128)(2,1)} collective-permute-done((bf16[512,1536]{0,1:T(8,128)(2,1)}, bf16[512,1536]{0,1:T(8,128)(2,1)}, u32[]{:S(2)}, u32[]{:S(2)}) %collective-permute-start.2) | collective-permute-done | bytes 1572896 | tf_op jit(solution)/shard_map/while/body/eval_jaxpr/ppermute | solution.py:12
  832.3 47.3 %conditional.6 = (f32[1024,1536]{1,0:T(8,128)}, f32[1024,80]{0,1:T(8,128)}, f32[1024]{0:T(1024)S(1)}, f32[768,512]{1,0:T(8,128)S(1)}, f32[768]{0:T(1024)S(1)}, /...) conditional(s32[]{:T(128)} %convert_element_type.177, () %tuple.147, (pred[]{:T(512)}, ...), branch_computations={%region_10.10_spmd, %region_11.13_spmd} | conditional | flops 12672174080 | bytes 166845824 | solution.py:261
  906.0 47.4 %conditional.6 = (f32[1024,1536]{1,0:T(8,128)}, f32[1024,80]{0,1:T(8,128)}, f32[1024]{0:T(1024)S(1)}, f32[768,512]{1,0:T(8,128)S(1)}, f32[768]{0:T(1024)S(1)}, /...) conditional(s32[]{:T(128)} %convert_element_type.177, () %tuple.147, (pred[]{:T(512)}, ...), branch_computations={%region_10.10_spmd, %region_11.13_spmd} | conditional | flops 12672174080 | bytes 166845824 | solution.py:261
  979.6 47.3 %conditional.6 = (f32[1024,1536]{1,0:T(8,128)}, f32[1024,80]{0,1:T(8,128)}, f32[1024]{0:T(1024)S(1)}, f32[768,512]{1,0:T(8,128)S(1)}, f32[768]{0:T(1024)S(1)}, /...) conditional(s32[]{:T(128)} %convert_element_type.177, () %tuple.147, (pred[]{:T(512)}, ...), branch_computations={%region_10.10_spmd, %region_11.13_spmd} | conditional | flops 12672174080 | bytes 166845824 | solution.py:261
  1053.3 47.3 %conditional.6 = (f32[1024,1536]{1,0:T(8,128)}, f32[1024,80]{0,1:T(8,128)}, f32[1024]{0:T(1024)S(1)}, f32[768,512]{1,0:T(8,128)S(1)}, f32[768]{0:T(1024)S(1)}, /...) conditional(s32[]{:T(128)} %convert_element_type.177, () %tuple.147, (pred[]{:T(512)}, ...), branch_computations={%region_10.10_spmd, %region_11.13_spmd} | conditional | flops 12672174080 | bytes 166845824 | solution.py:261
  1146.2 22.3 %all-reduce.7 = (bf16[1024]{0:T(1024)(128)(2,1)}, bf16[768]{0:T(1024)(128)(2,1)}) all-reduce(bf16[1024]{0:T(1024)(128)(2,1)S(1)} %convert_element_type.145, bf16[768]{0:T(1024)(128)(2,1)S(1)} %convert_element_type.147), channel_id=5, replica_groups=mesh['dp'=8,'layer'=4] {'dp'}, use_global_device_ids=true, to_apply=%region_25.26.clone | all-reduce | flops 1792 | bytes 7168
  1186.6 63.9 %reduce-scatter.11.cloned.1.call-done = bf16[96,512]{1,0:T(8,128)(2,1)} async-done(((bf16[768,512]{1,0:T(8,128)(2,1)}), bf16[96,512]{1,0:T(8,128)(2,1)}) %reduce-scatter.11.cloned.1.call-update) | async-done | bytes 98320 | tf_op jit(solution)/shard_map/reduce_scatter | solution.py:290
  1252.1 26.5 %reduce-scatter.7.cloned.1.call-done = bf16[97,1536]{1,0:T(8,128)(2,1)} async-done(((bf16[97,6144]{1,0:T(8,128)(2,1)}), bf16[97,1536]{1,0:T(8,128)(2,1)}) %reduce-scatter.7.cloned.1.call-update) | async-done | bytes 298000 | tf_op jit(solution)/shard_map/reduce_scatter | solution.py:318
  1285.1 42.0 %all-reduce.6 = (f32[8,8]{1,0:T(8,128)}, f32[512,4]{0,1:T(4,128)}, f32[512]{0:T(512)}, f32[8,768]{1,0:T(8,128)}, f32[8]{0:T(128)}) all-reduce(f32[8,8]{1,0:T(8,128)S(1)} %scatter_fusion, f32[512,4]{0,1:T(4,128)S(1)} %fusion.57, f32[512]{0:T(512)S(1)} %broadcast_multiply_fusion, ...), channel_id=1, replica_groups=mesh['dp'=8,'layer'=4] {'dp','layer'}, use_global_device_ids=true, to_apply=%region_19.20 | all-reduce | flops 8776 | bytes 70208 | tf_op jit(solution)/shard_map/psum | solution.py:333
  1329.4 28.3 %reduce-scatter.9.cloned.1.call-done = bf16[128,1536]{1,0:T(8,128)(2,1)} async-done(((bf16[1024,1536]{1,0:T(8,128)(2,1)}), bf16[128,1536]{1,0:T(8,128)(2,1)}) %reduce-scatter.9.cloned.1.call-update) | async-done | bytes 393232 | tf_op jit(solution)/shard_map/reduce_scatter | solution.py:281
  (728 shorter events, 1029.7 us)
Async XLA Ops:
  7.2 1177.9 %reduce-scatter.13.cloned.1.call-start = ((), (), s32[]{:S(2)}) async-start(), calls=%async_computation.7 | async-start | bytes 294912
  89.5 52.1 %collective-permute-start = (bf16[512,1536]{0,1:T(8,128)(2,1)}, bf16[512,1536]{0,1:T(8,128)(2,1)}, u32[]{:S(2)}, u32[]{:S(2)}) collective-permute-start(bf16[512,1536]{0,1:T(8,128)(2,1)} %get-tuple-element.1744), channel_id=1, source_target_pairs={{0,1},{1,2},{2,3},{4,5},{5,6},{6,7},{8,9},{9,10},{10,11},{12,13},{... | collective-permute-start | bytes 4718600 | tf_op jit(solution)/shard_map/while/body/eval_jaxpr/ppermute | solution.py:12
  96.6 45.0 %collective-permute-start.1 = (f32[256,1536]{0,1:T(8,128)}, f32[256,1536]{0,1:T(8,128)}, u32[]{:S(2)}, u32[]{:S(2)}) collective-permute-start(f32[256,1536]{0,1:T(8,128)} %get-tuple-element.1745), channel_id=1, source_target_pairs={{0,1},{1,2},{2,3},{4,5},{5,6},{6,7},{8,9},{9,10},{10,11},{12,13},{... | collective-permute-start | bytes 4718600 | tf_op jit(solution)/shard_map/while/body/eval_jaxpr/ppermute | solution.py:12
  177.4 52.0 %collective-permute-start = (bf16[512,1536]{0,1:T(8,128)(2,1)}, bf16[512,1536]{0,1:T(8,128)(2,1)}, u32[]{:S(2)}, u32[]{:S(2)}) collective-permute-start(bf16[512,1536]{0,1:T(8,128)(2,1)} %get-tuple-element.1744), channel_id=1, source_target_pairs={{0,1},{1,2},{2,3},{4,5},{5,6},{6,7},{8,9},{9,10},{10,11},{12,13},{... | collective-permute-start | bytes 4718600 | tf_op jit(solution)/shard_map/while/body/eval_jaxpr/ppermute | solution.py:12
  184.5 44.9 %collective-permute-start.1 = (f32[256,1536]{0,1:T(8,128)}, f32[256,1536]{0,1:T(8,128)}, u32[]{:S(2)}, u32[]{:S(2)}) collective-permute-start(f32[256,1536]{0,1:T(8,128)} %get-tuple-element.1745), channel_id=1, source_target_pairs={{0,1},{1,2},{2,3},{4,5},{5,6},{6,7},{8,9},{9,10},{10,11},{12,13},{... | collective-permute-start | bytes 4718600 | tf_op jit(solution)/shard_map/while/body/eval_jaxpr/ppermute | solution.py:12
  265.2 52.0 %collective-permute-start = (bf16[512,1536]{0,1:T(8,128)(2,1)}, bf16[512,1536]{0,1:T(8,128)(2,1)}, u32[]{:S(2)}, u32[]{:S(2)}) collective-permute-start(bf16[512,1536]{0,1:T(8,128)(2,1)} %get-tuple-element.1744), channel_id=1, source_target_pairs={{0,1},{1,2},{2,3},{4,5},{5,6},{6,7},{8,9},{9,10},{10,11},{12,13},{... | collective-permute-start | bytes 4718600 | tf_op jit(solution)/shard_map/while/body/eval_jaxpr/ppermute | solution.py:12
  272.2 45.0 %collective-permute-start.1 = (f32[256,1536]{0,1:T(8,128)}, f32[256,1536]{0,1:T(8,128)}, u32[]{:S(2)}, u32[]{:S(2)}) collective-permute-start(f32[256,1536]{0,1:T(8,128)} %get-tuple-element.1745), channel_id=1, source_target_pairs={{0,1},{1,2},{2,3},{4,5},{5,6},{6,7},{8,9},{9,10},{10,11},{12,13},{... | collective-permute-start | bytes 4718600 | tf_op jit(solution)/shard_map/while/body/eval_jaxpr/ppermute | solution.py:12
  353.0 52.1 %collective-permute-start = (bf16[512,1536]{0,1:T(8,128)(2,1)}, bf16[512,1536]{0,1:T(8,128)(2,1)}, u32[]{:S(2)}, u32[]{:S(2)}) collective-permute-start(bf16[512,1536]{0,1:T(8,128)(2,1)} %get-tuple-element.1744), channel_id=1, source_target_pairs={{0,1},{1,2},{2,3},{4,5},{5,6},{6,7},{8,9},{9,10},{10,11},{12,13},{... | collective-permute-start | bytes 4718600 | tf_op jit(solution)/shard_map/while/body/eval_jaxpr/ppermute | solution.py:12
  360.1 45.1 %collective-permute-start.1 = (f32[256,1536]{0,1:T(8,128)}, f32[256,1536]{0,1:T(8,128)}, u32[]{:S(2)}, u32[]{:S(2)}) collective-permute-start(f32[256,1536]{0,1:T(8,128)} %get-tuple-element.1745), channel_id=1, source_target_pairs={{0,1},{1,2},{2,3},{4,5},{5,6},{6,7},{8,9},{9,10},{10,11},{12,13},{... | collective-permute-start | bytes 4718600 | tf_op jit(solution)/shard_map/while/body/eval_jaxpr/ppermute | solution.py:12
  424.1 52.1 %collective-permute-start = (bf16[512,1536]{0,1:T(8,128)(2,1)}, bf16[512,1536]{0,1:T(8,128)(2,1)}, u32[]{:S(2)}, u32[]{:S(2)}) collective-permute-start(bf16[512,1536]{0,1:T(8,128)(2,1)} %get-tuple-element.1744), channel_id=1, source_target_pairs={{0,1},{1,2},{2,3},{4,5},{5,6},{6,7},{8,9},{9,10},{10,11},{12,13},{... | collective-permute-start | bytes 4718600 | tf_op jit(solution)/shard_map/while/body/eval_jaxpr/ppermute | solution.py:12
  433.0 43.2 %collective-permute-start.1 = (f32[256,1536]{0,1:T(8,128)}, f32[256,1536]{0,1:T(8,128)}, u32[]{:S(2)}, u32[]{:S(2)}) collective-permute-start(f32[256,1536]{0,1:T(8,128)} %get-tuple-element.1745), channel_id=1, source_target_pairs={{0,1},{1,2},{2,3},{4,5},{5,6},{6,7},{8,9},{9,10},{10,11},{12,13},{... | collective-permute-start | bytes 4718600 | tf_op jit(solution)/shard_map/while/body/eval_jaxpr/ppermute | solution.py:12
  495.2 56.1 %collective-permute-start = (bf16[512,1536]{0,1:T(8,128)(2,1)}, bf16[512,1536]{0,1:T(8,128)(2,1)}, u32[]{:S(2)}, u32[]{:S(2)}) collective-permute-start(bf16[512,1536]{0,1:T(8,128)(2,1)} %get-tuple-element.1744), channel_id=1, source_target_pairs={{0,1},{1,2},{2,3},{4,5},{5,6},{6,7},{8,9},{9,10},{10,11},{12,13},{... | collective-permute-start | bytes 4718600 | tf_op jit(solution)/shard_map/while/body/eval_jaxpr/ppermute | solution.py:12
  504.0 47.4 %collective-permute-start.1 = (f32[256,1536]{0,1:T(8,128)}, f32[256,1536]{0,1:T(8,128)}, u32[]{:S(2)}, u32[]{:S(2)}) collective-permute-start(f32[256,1536]{0,1:T(8,128)} %get-tuple-element.1745), channel_id=1, source_target_pairs={{0,1},{1,2},{2,3},{4,5},{5,6},{6,7},{8,9},{9,10},{10,11},{12,13},{... | collective-permute-start | bytes 4718600 | tf_op jit(solution)/shard_map/while/body/eval_jaxpr/ppermute | solution.py:12
  570.3 52.0 %collective-permute-start = (bf16[512,1536]{0,1:T(8,128)(2,1)}, bf16[512,1536]{0,1:T(8,128)(2,1)}, u32[]{:S(2)}, u32[]{:S(2)}) collective-permute-start(bf16[512,1536]{0,1:T(8,128)(2,1)} %get-tuple-element.1744), channel_id=1, source_target_pairs={{0,1},{1,2},{2,3},{4,5},{5,6},{6,7},{8,9},{9,10},{10,11},{12,13},{... | collective-permute-start | bytes 4718600 | tf_op jit(solution)/shard_map/while/body/eval_jaxpr/ppermute | solution.py:12
  577.4 44.9 %collective-permute-start.1 = (f32[256,1536]{0,1:T(8,128)}, f32[256,1536]{0,1:T(8,128)}, u32[]{:S(2)}, u32[]{:S(2)}) collective-permute-start(f32[256,1536]{0,1:T(8,128)} %get-tuple-element.1745), channel_id=1, source_target_pairs={{0,1},{1,2},{2,3},{4,5},{5,6},{6,7},{8,9},{9,10},{10,11},{12,13},{... | collective-permute-start | bytes 4718600 | tf_op jit(solution)/shard_map/while/body/eval_jaxpr/ppermute | solution.py:12
  701.0 77.2 %collective-permute-start.3 = (bf16[256,1536]{0,1:T(8,128)(2,1)}, bf16[256,1536]{0,1:T(8,128)(2,1)}, u32[]{:S(2)}, u32[]{:S(2)}) collective-permute-start(bf16[256,1536]{0,1:T(8,128)(2,1)} %bitcast_select_fusion.11), channel_id=1, source_target_pairs={{1,0},{2,1},{3,2},{5,4},{6,5},{7,6},{9,8},{10,9},{11,10},{13,12},{... | collective-permute-start | bytes 2359304 | tf_op jit(solution)/shard_map/while/body/eval_jaxpr/ppermute | solution.py:12
  708.8 119.9 %collective-permute-start.2 = (bf16[512,1536]{0,1:T(8,128)(2,1)}, bf16[512,1536]{0,1:T(8,128)(2,1)}, u32[]{:S(2)}, u32[]{:S(2)}) collective-permute-start(bf16[512,1536]{0,1:T(8,128)(2,1)} %get-tuple-element.1776), channel_id=1, source_target_pairs={{1,0},{2,1},{3,2},{5,4},{6,5},{7,6},{9,8},{10,9},{11,10},{13,12},{... | collective-permute-start | bytes 4718600 | tf_op jit(solution)/shard_map/while/body/eval_jaxpr/ppermute | solution.py:12
  831.0 69.0 %collective-permute-start.3 = (bf16[256,1536]{0,1:T(8,128)(2,1)}, bf16[256,1536]{0,1:T(8,128)(2,1)}, u32[]{:S(2)}, u32[]{:S(2)}) collective-permute-start(bf16[256,1536]{0,1:T(8,128)(2,1)} %bitcast_select_fusion.11), channel_id=1, source_target_pairs={{1,0},{2,1},{3,2},{5,4},{6,5},{7,6},{9,8},{10,9},{11,10},{13,12},{... | collective-permute-start | bytes 2359304 | tf_op jit(solution)/shard_map/while/body/eval_jaxpr/ppermute | solution.py:12
  904.7 69.1 %collective-permute-start.3 = (bf16[256,1536]{0,1:T(8,128)(2,1)}, bf16[256,1536]{0,1:T(8,128)(2,1)}, u32[]{:S(2)}, u32[]{:S(2)}) collective-permute-start(bf16[256,1536]{0,1:T(8,128)(2,1)} %bitcast_select_fusion.11), channel_id=1, source_target_pairs={{1,0},{2,1},{3,2},{5,4},{6,5},{7,6},{9,8},{10,9},{11,10},{13,12},{... | collective-permute-start | bytes 2359304 | tf_op jit(solution)/shard_map/while/body/eval_jaxpr/ppermute | solution.py:12
  978.3 69.0 %collective-permute-start.3 = (bf16[256,1536]{0,1:T(8,128)(2,1)}, bf16[256,1536]{0,1:T(8,128)(2,1)}, u32[]{:S(2)}, u32[]{:S(2)}) collective-permute-start(bf16[256,1536]{0,1:T(8,128)(2,1)} %bitcast_select_fusion.11), channel_id=1, source_target_pairs={{1,0},{2,1},{3,2},{5,4},{6,5},{7,6},{9,8},{10,9},{11,10},{13,12},{... | collective-permute-start | bytes 2359304 | tf_op jit(solution)/shard_map/while/body/eval_jaxpr/ppermute | solution.py:12
  1052.0 69.0 %collective-permute-start.3 = (bf16[256,1536]{0,1:T(8,128)(2,1)}, bf16[256,1536]{0,1:T(8,128)(2,1)}, u32[]{:S(2)}, u32[]{:S(2)}) collective-permute-start(bf16[256,1536]{0,1:T(8,128)(2,1)} %bitcast_select_fusion.11), channel_id=1, source_target_pairs={{1,0},{2,1},{3,2},{5,4},{6,5},{7,6},{9,8},{10,9},{11,10},{13,12},{... | collective-permute-start | bytes 2359304 | tf_op jit(solution)/shard_map/while/body/eval_jaxpr/ppermute | solution.py:12
  1123.2 127.3 %reduce-scatter.11.cloned.1.call-start = ((), (), s32[]{:S(2)}) async-start(), calls=%async_computation.6 | async-start | bytes 884736 | tf_op jit(solution)/shard_map/reduce_scatter | solution.py:290
  1125.7 152.9 %reduce-scatter.7.cloned.1.call-start = ((), (), s32[]{:S(2)}) async-start(), calls=%async_computation.4 | async-start | bytes 1597440 | tf_op jit(solution)/shard_map/reduce_scatter | solution.py:318
  1136.6 221.1 %reduce-scatter.9.cloned.1.call-start = ((), (), s32[]{:S(2)}) async-start(), calls=%async_computation.5 | async-start | bytes 3538944 | tf_op jit(solution)/shard_map/reduce_scatter | solution.py:281
  (137 other events, 2687.3 us)
Sparse Core Ops, SparseCore 0:
  1123.4 61.6 reduce-scatter.12
  1189.0 61.4 reduce-scatter.10
  1253.3 25.2 reduce-scatter.6
  1282.0 75.5 reduce-scatter.8
where the time goes:
time: 1380 us; the launch traced here: 1370 us
  local copies, waits for them, and re-layouts  414 us (30%)
  other arithmetic  358 us (26%)
  waiting for transfers between devices  229 us (17%)
  matrix products  219 us (16%)
  blocking collectives  64.3 us (5%)
  starting transfers between devices  61.9 us (4%)
  between operations  16.6 us (1%)
    dynamic_slice x78, local copies, waits for them, and re-layouts, pick(): lax.dynamic_index_in_dim(stack, micro_slot, axis_number, keepdims=False)  158 us
    dynamic_update_slice x49, local copies, waits for them, and re-layouts, place_in(): lax.dynamic_update_index_in_dim(stack, jnp.where(flag, piece, old_piece),...  146 us
    broadcast_in_dim x28, other arithmetic, place_in(): lax.dynamic_update_index_in_dim(stack, jnp.where(flag, piece, old_piece),...  135 us
    dot_general x24, matrix products, contract(): lax.dot_general(first, second, (((first_dim,), (second_dim,)), ((), ())),...  112 us
    ppermute x28, waiting for transfers between devices, shifted(): return lax.ppermute(block, axis, route)  109 us
    add x35, other arithmetic, back_step(): running + addend  72.5 us
    reduce_scatter x1, waiting for transfers between devices, per_device(): lax.psum_scatter(totals[3].astype(jnp.bfloat16), 'dp', scatter_dimension=...  63.9 us
    ppermute x28, starting transfers between devices, shifted(): return lax.ppermute(block, axis, route)  61.8 us
  transfers between devices with their start and end apart: 32, of which 9 were waited for; matrix products, arithmetic and copies ran while one was open for 51% of the time, Pallas kernels for 0%

commit v1 on v0

v1 whole, which is shorter than its diff:
```python
import functools

import jax
import jax.numpy as jnp
from jax import lax
from jax.experimental import pallas as pl
from jax.experimental.pallas import tpu as pltpu
from jax.sharding import PartitionSpec as P

BF = jnp.bfloat16
F32 = jnp.float32
LANES = 128
MISC = 48
MIB = 1 << 20
highest = lax.Precision.HIGHEST
VMEM = pltpu.VMEM
ANY = pl.ANY


def mm(first, second, first_dim=1, second_dim=0):
    return lax.dot_general(
        first, second, (((first_dim,), (second_dim,)), ((), ())), preferred_element_type=F32
    )


def split_high_low(values):
    high = values.astype(BF)
    return high, (values - high.astype(F32)).astype(BF)


def kept(rows, cols, dtype=BF):
    return pltpu.HBM((rows, cols), dtype)


def whole(space=VMEM):
    return pl.BlockSpec(memory_space=space)


def call(body, name, out_shape, scratch, grid=None, in_specs=None, out_specs=None, flops=0, nbytes=0, vmem=24):
    return pl.pallas_call(
        body,
        name=name,
        out_shape=out_shape,
        grid_spec=pltpu.PrefetchScalarGridSpec(
            num_scalar_prefetch=1,
            grid=grid or (1,),
            in_specs=in_specs,
            out_specs=out_specs,
            scratch_shapes=scratch,
        ),
        compiler_params=pltpu.CompilerParams(vmem_limit_bytes=vmem * MIB),
        cost_estimate=pl.CostEstimate(
            flops=int(flops), bytes_accessed=int(nbytes), transcendentals=0
        ),
    )


class Sizes:
    def __init__(self, args, cycle, data):
        (audio, mel, lengths, _, _, _, start_weight, _, in_weight, _, _, mix_weight) = args[:12]
        self.cycle, self.data = cycle, data
        self.micro, self.utts = lengths.shape
        self.copies = cycle // self.micro
        assert self.copies * self.micro == cycle
        self.frames = audio.shape[1] // self.micro
        self.group = audio.shape[0]
        self.half = self.group // 2
        self.mel = mel.shape[0]
        self.res = start_weight.shape[0]
        self.gate = in_weight.shape[1]
        self.taps = in_weight.shape[2]
        self.mixed_rows = mix_weight.shape[1]
        self.skip = self.mixed_rows - self.res
        self.ones = self.mel
        self.tap_rows = 3 * self.half + 2
        self.first = self.mel + 2
        self.x_rows = -(-(self.first + 3 * self.tap_rows) // LANES) * LANES
        self.all_rows = self.taps + self.x_rows
        self.pack_misc = self.res
        self.pack_cond = self.res + MISC
        self.me_rows = self.res + LANES
        self.cond_blocks = self.res // self.x_rows
        self.cond_rows = self.gate // self.cond_blocks
        self.pack_rows = self.pack_cond + self.cond_rows
        self.blocks = self.gate // LANES
        self.m_rows = self.mixed_rows // self.blocks
        self.m_fold = self.res // LANES
        self.m_pack = self.m_rows * self.m_fold
        self.share_first = self.x_rows + self.m_pack
        self.share_rows = self.taps + self.share_first
        self.direct = cycle == 4 and data == self.blocks
        self.bits = data.bit_length() - 1

    def tap(self, number):
        return self.first + number * self.tap_rows


def prepare_weights(z, in_w, cond, gate_bias, mix, mix_bias, start, end_w):
    def body(s_ref, in_ref, cond_ref, gb_ref, mix_ref, mb_ref, start_ref, end_ref, pack_ref, sx_ref, acc, in_v, sem):
        start_high, start_low = split_high_low(start_ref[...])
        start_pair = jnp.concatenate([start_high.astype(F32), start_low.astype(F32)], axis=0).astype(BF)
        in_copy = pltpu.make_async_copy(in_ref, in_v, sem)

        @pl.when(s_ref[0] == 0)
        def _():
            in_copy.start()

        col = lax.broadcasted_iota(jnp.int32, (8, z.x_rows), 1)

        row16 = lax.broadcasted_iota(jnp.int32, (16, z.x_rows), 0)
        col16 = lax.broadcasted_iota(jnp.int32, (16, z.x_rows), 1)

        def spread(tap):
            base, h = z.tap(tap), z.half
            spot = jnp.where(col16 < base + 3 * h, lax.rem(col16 - base + 3 * h, h), h)
            inside = (col16 >= base) & (col16 < base + z.tap_rows)
            hit = (inside & ((row16 & 7) == spot)).astype(F32).astype(BF)
            return mm(start_pair, hit, 0, 0)

        def is_low(tap):
            base = z.tap(tap)
            return ((col >= base + 2 * z.half) & (col < base + 3 * z.half)) | (col == base + 3 * z.half + 1)

        def choose(values, low_cols):
            high = values.astype(BF).astype(F32)
            return jnp.where(low_cols, values - high, high).astype(BF)

        eye = (
            lax.broadcasted_iota(jnp.int32, (z.mel, z.x_rows), 0)
            == lax.broadcasted_iota(jnp.int32, (z.mel, z.x_rows), 1)
        ).astype(F32).astype(BF)
        bias = gb_ref[...]
        bias_high = bias.astype(BF).astype(F32)
        bias_rows = jnp.concatenate([bias_high, bias - bias_high, jnp.zeros((14, z.gate), F32)], axis=0)
        pick = (((row16 == 0) & (col16 == z.ones)) | ((row16 == 1) & (col16 == z.ones + 1))).astype(F32)
        acc[...] = mm(cond_ref[...], eye) + mm(bias_rows.astype(BF), pick.astype(BF), 0, 0)
        middle = spread(1)
        end_res = end_ref[:, 0 : z.res]
        high, low = split_high_low(middle)
        ends_start = mm(end_res, high) + mm(end_res, low)
        sx_ref[0 : z.res, :] = choose(middle, is_low(1)[0:1, :])
        sx_ref[z.res :, :] = jnp.concatenate([choose(ends_start, is_low(1)).astype(F32), jnp.zeros((8, z.x_rows), F32)], axis=0).astype(BF)
        pack_ref[0 : z.res, :] = mix_ref[0 : z.res, :]
        ends = mm(end_ref[...], mix_ref[...])
        ends_high = ends.astype(BF).astype(F32)
        bias_end = jnp.sum(end_ref[...].astype(F32) * mb_ref[...], axis=1, keepdims=True)
        bias_end = jnp.broadcast_to(bias_end, (z.group, z.res))
        bias_end_high = bias_end.astype(BF).astype(F32)
        own = mb_ref[:, 0 : z.res]
        own_high = own.astype(BF).astype(F32)
        pack_ref[z.pack_misc : z.pack_misc + 16, :] = jnp.concatenate([ends_high, ends - ends_high], axis=0).astype(BF)
        pack_ref[z.pack_misc + 16 : z.pack_misc + 32, :] = jnp.concatenate(
            [bias_end_high, bias_end - bias_end_high], axis=0
        ).astype(BF)
        pack_ref[z.pack_misc + 32 : z.pack_misc + 48, :] = jnp.concatenate(
            [own_high, own - own_high, jnp.zeros((14, z.res), F32)], axis=0
        ).astype(BF)

        @pl.when(s_ref[0] == 0)
        def _():
            in_copy.wait()
            for tap in range(3):
                high, low = split_high_low(spread(tap))
                block = in_v[:, tap * z.res : (tap + 1) * z.res]
                acc[...] += mm(block, high) + mm(block, low)

        low_cols = (is_low(0) | is_low(1) | is_low(2))[0:1, :]
        cond_x = choose(acc[...], low_cols)
        for j in range(z.cond_blocks):
            pack_ref[z.pack_cond :, j * z.x_rows : (j + 1) * z.x_rows] = cond_x[
                j * z.cond_rows : (j + 1) * z.cond_rows
            ]

    return call(
        body,
        "prepare_weights",
        (
            kept(z.pack_rows, z.res),
            jax.ShapeDtypeStruct((z.res + 16, z.x_rows), BF),
        ),
        [pltpu.VMEM((z.gate, z.x_rows), F32), pltpu.VMEM((z.gate, z.taps), BF), pltpu.SemaphoreType.DMA],
        in_specs=[whole(ANY)] + [whole()] * 6,
        out_specs=(whole(), whole()),
        flops=2 * z.gate * z.taps * z.x_rows,
        nbytes=6 * MIB,
    )


def prepare_frames(z):
    def body(s_ref, len_ref, audio_ref, mel_ref, lu_ref, x_ref, mixed_ref, mask_ref, turned_ref, matrix_ref, tall):
        lu = lu_ref[...]
        r = lax.broadcasted_iota(jnp.int32, lu.shape, 0)
        c = lax.broadcasted_iota(jnp.int32, lu.shape, 1)
        lower = jnp.where(r > c, lu, 0.0) + jnp.where(r == c, 1.0, 0.0)
        upper = jnp.where(r < c, lu, 0.0) + jnp.where(r == c, jnp.exp(lu), 0.0)
        matrix = lower[:, 0:1] * upper[0:1, :]
        for k in range(1, z.group):
            matrix = matrix + lower[:, k : k + 1] * upper[k : k + 1, :]
        matrix_ref[...] = matrix
        mixed = matrix[:, 0:1] * audio_ref[0:1, :]
        for k in range(1, z.group):
            mixed = mixed + matrix[:, k : k + 1] * audio_ref[k : k + 1, :]
        mixed_ref[...] = mixed
        place = lax.broadcasted_iota(jnp.int32, (16, z.frames), 1)
        begin = jnp.int32(0)
        left = jnp.zeros((16, z.frames), jnp.int32)
        right = jnp.zeros((16, z.frames), jnp.int32)
        for u in range(z.utts):
            size = len_ref[s_ref[2], u]
            inside = (place >= begin) & (place < begin + size)
            left = jnp.where(inside, place - begin, left)
            right = jnp.where(inside, begin + size - 1 - place, right)
            begin = begin + size
        for l in range(z.cycle):
            mask_ref[l, 0:16, :] = (left >= 2**l).astype(F32).astype(BF)
            mask_ref[l, 16:32, :] = (right >= 2**l).astype(F32).astype(BF)
        tall[...] = jnp.zeros_like(tall)
        for l in range(z.cycle):
            tall[2 * l : 2 * l + 1, :] = (left >= 2**l).astype(F32)[0:1]
            tall[2 * l + 1 : 2 * l + 2, :] = (right >= 2**l).astype(F32)[0:1]
        turned_ref[...] = tall[...].T
        high = mixed.astype(BF).astype(F32)
        low = (mixed - high).astype(BF).astype(F32)
        tall[...] = jnp.zeros_like(tall)
        tall[0 : z.mel, :] = mel_ref[...].astype(F32)
        tall[z.ones : z.ones + 2, :] = jnp.ones((2, z.frames), F32)
        masks = ((left >= 1).astype(F32)[0:8], jnp.ones((8, z.frames), F32), (right >= 1).astype(F32)[0:8])
        for tap in range(3):
            shift = (1, 0, z.frames - 1)[tap]
            moved_high = (pltpu.roll(high, shift, axis=1) if shift else high) * masks[tap]
            moved_low = (pltpu.roll(low, shift, axis=1) if shift else low) * masks[tap]
            base = z.tap(tap)
            h = z.half
            tall[base : base + h, :] = moved_high[0:h]
            tall[base + h : base + 2 * h, :] = moved_low[0:h]
            tall[base + 2 * h : base + 3 * h, :] = moved_high[0:h]
            tall[base + 3 * h : base + 3 * h + 2, :] = masks[tap][0:2]
        x_ref[...] = tall[...].astype(BF)

    def column(rows):
        return pl.BlockSpec((rows, z.frames), lambda i, s: (0, s[2]))

    return call(
        body,
        "prepare_frames",
        (
            kept(z.x_rows, z.frames),
            jax.ShapeDtypeStruct((z.group, z.frames), F32),
            pltpu.HBM((z.cycle, 32, z.frames), BF),
            kept(z.frames, z.x_rows, F32),
            jax.ShapeDtypeStruct((z.group, z.group), F32),
        ),
        [pltpu.VMEM((z.x_rows, z.frames), F32)],
        in_specs=[whole(pltpu.SMEM), column(z.group), column(z.mel), whole()],
        out_specs=(whole(),) * 5,
        flops=1e6,
        nbytes=2 * MIB,
    )


def taps_copies(z, s_ref, sources, layer, target, sem):
    if len(sources) == 1:
        return [pltpu.make_async_copy(sources[0].at[layer], target, sem)], None
    copy = pltpu.make_async_copy
    if len(sources) == 4:
        return [[copy(source, target, sem)] for source in sources], s_ref[0] ^ layer
    own, near, far, beside, cross, cross_beside = sources
    rows = z.gate // 2
    x = s_ref[1] & 1
    mine = target.at[pl.ds(pl.multiple_of(x * rows, rows), rows)]
    other = target.at[pl.ds(pl.multiple_of((1 - x) * rows, rows), rows)]
    slots = [
        [copy(own, target, sem)],
        [copy(near, target, sem)],
        [copy(far, mine, sem), copy(beside, other, sem)],
        [copy(cross, mine, sem), copy(cross_beside, other, sem)],
    ]
    return slots, s_ref[0] ^ layer


def pack_copies(z, s_ref, packs, layer, me, wide, column, sems):
    def of(ref):
        conds = [
            pltpu.make_async_copy(
                ref.at[pl.ds(z.pack_cond, z.cond_rows), pl.ds(j * z.x_rows, z.x_rows)],
                wide.at[pl.ds(j * z.cond_rows, z.cond_rows), pl.ds(column, z.x_rows)],
                sems.at[0],
            )
            for j in range(z.cond_blocks)
        ]
        return conds + [
            pltpu.make_async_copy(ref.at[pl.ds(0, z.pack_cond)], me.at[pl.ds(0, z.pack_cond)], sems.at[1])
        ]

    if len(packs) == 1:
        return of(packs[0].at[layer]), None
    return [of(ref) for ref in packs], s_ref[0] ^ layer


def each(copies, action):
    chosen, slot = copies
    if slot is None:
        for copy in chosen:
            getattr(copy, action)()
        return
    for number, group in enumerate(chosen):

        @pl.when(slot == number)
        def _():
            for copy in group:
                getattr(copy, action)()


def fill_taps(z, taps, mask, layer):
    dilation = 2**layer
    rows = 32

    def one(i, _):
        begin = pl.multiple_of(i * rows, rows)
        block = taps[pl.ds(z.res + begin, rows), :]
        before = pltpu.roll(block, dilation, axis=1).reshape(rows // 16, 16, z.frames)
        after = pltpu.roll(block, z.frames - dilation, axis=1).reshape(rows // 16, 16, z.frames)
        taps[pl.ds(begin, rows), :] = (before * mask[0:16, :][None]).reshape(rows, z.frames)
        taps[pl.ds(2 * z.res + begin, rows), :] = (after * mask[16:32, :][None]).reshape(rows, z.frames)
        return 0

    lax.fori_loop(0, z.res // rows, one, 0)


class Copies:
    def __init__(self, sems):
        self.sems, self.used = sems, 0

    def start(self, source, target):
        copy = pltpu.make_async_copy(source, target, self.sems.at[self.used])
        self.used += 1
        copy.start()
        return copy

    def weights(self, z, s_ref, sources, packs, layer, wide, me, column):
        pack = pack_copies(z, s_ref, packs, layer, me, wide, column, self.sems.at[pl.ds(self.used, 2)])
        self.used += 2
        each(pack, "start")
        if not layer:
            return pack, None
        taps = taps_copies(z, s_ref, sources, layer, wide.at[:, pl.ds(0, z.taps)], self.sems.at[self.used])
        self.used += 1
        each(taps, "start")
        return pack, taps


def gate_parts(first, second):
    tanh = jnp.tanh(first)
    sig = 0.5 * jnp.tanh(0.5 * second) + 0.5
    gated = tanh * sig
    return gated.astype(BF), (sig - gated * tanh).astype(BF), (gated - gated * sig).astype(BF)


def bias_column(z, me):
    row = lax.broadcasted_iota(jnp.int32, (16, LANES), 0)
    pick = (row < 2).astype(F32).astype(BF)
    return mm(me[z.pack_misc + 32 : z.pack_misc + 48, :], pick, 0, 0)[:, 0:1]


def bias_end(z, me):
    rows = me[z.pack_misc + 16 : z.pack_misc + 32, :].astype(F32)
    return (rows[0 : z.group] + rows[z.group : 2 * z.group])[:, 0:1]


def forward_parts(z, layer, wide, taps, me, pre, add_end, start_of, save, gated_v, fa_v, fb_v, out_v, total):
    width = pre.shape[2]
    parts = z.frames // width
    mix_rows = 0 if layer == z.cycle - 1 else z.res
    add_stream = bias_column(z, me) if mix_rows else None

    def product(part):
        pre[part % 2, :, :] = mm(wide[...], taps[:, part * width : (part + 1) * width])

    product(0)
    for part in range(parts):
        if part + 1 < parts:
            product(part + 1)
        here = slice(part * width, (part + 1) * width)
        gated, fa, fb = gate_parts(pre[part % 2, 0 : z.res, :], pre[part % 2, z.res :, :])
        gated_v[:, here] = gated
        fa_v[here, :] = fa.T
        fb_v[here, :] = fb.T
        branch = mm(me[z.res - mix_rows : z.res + 16, :], gated)
        ends = branch[mix_rows : mix_rows + z.group] + branch[mix_rows + z.group :] + add_end
        if start_of is None:
            total[:, here] = total[:, here] + ends
        else:
            start = start_of(here)
            total[:, here] = ends + start[z.res : z.res + z.group]
        if mix_rows:
            stream = taps[z.res : 2 * z.res, here].astype(F32) if start_of is None else start[0 : z.res]
            if start_of is not None:
                stream = stream.astype(BF).astype(F32)
            out_v[:, here] = (stream + branch[0 : z.res] + add_stream).astype(BF)
        save(part)


def forward_group(z, n_sources, n_packs):
    width = 256
    parts = z.frames // width
    count = z.cycle - 1

    def body(s_ref, *refs):
        refs = list(refs)
        take = lambda n: [refs.pop(0) for _ in range(n)]
        sources, packs = take(n_sources), take(n_packs)
        (x_ref, mask_ref, sx_ref) = take(3)
        kept_refs = [take(4) for _ in range(count)]
        (total,) = take(1)
        (wides, first_wide, all_taps, x_v, mes, pre, gated_vs, fa_vs, fb_vs, masks, sems) = take(11)
        copies = Copies(sems)
        pending = {0: copies.weights(z, s_ref, sources, packs, 0, first_wide, mes.at[0], 0)}
        x_in = copies.start(x_ref, x_v)
        mask_in = copies.start(mask_ref, masks)
        x_taps = [copies.start(x_ref, all_taps.at[k, pl.ds(z.taps, z.x_rows)]) for k in range(2)]

        def bring(layer):
            k = layer % 2
            pending[layer] = copies.weights(z, s_ref, sources, packs, layer, wides.at[k], mes.at[k], z.taps)

        if count > 1:
            bring(1)
        x_in.wait()
        saves = {}
        for layer in range(count):
            k = layer % 2
            pack, taps_in = pending[layer]
            if layer and layer + 1 < count:
                bring(layer + 1)
            me = mes.at[k]
            taps = all_taps.at[k] if layer else x_v
            wide = wides.at[k] if layer else first_wide
            if layer == 1:
                mask_in.wait()
                for copy in x_taps:
                    copy.wait()
            if layer:
                fill_taps(z, taps, masks.at[layer], layer)
            each(pack, "wait")
            if layer:
                each(taps_in, "wait")
            for done in (layer - 1, layer - 2):
                for copy in saves.pop(done, []):
                    copy.wait()
            gated_v, fa_v, fb_v = gated_vs.at[k], fa_vs.at[k], fb_vs.at[k]
            out_v = all_taps.at[1 - k, pl.ds(z.res, z.res)]
            gated_ref, fa_ref, fb_ref, out_ref = kept_refs[layer]
            mine = saves[layer] = []

            def save(part):
                at = pl.ds(part * width, width)
                mine.append(copies.start(gated_v.at[:, at], gated_ref.at[:, at]))
                mine.append(copies.start(fa_v.at[at], fa_ref.at[at]))
                mine.append(copies.start(fb_v.at[at], fb_ref.at[at]))
                mine.append(copies.start(out_v.at[:, at], out_ref.at[:, at]))

            start_of = None if layer else (lambda here: mm(sx_ref[...], x_v[:, here]))
            forward_parts(
                z, layer, wide, taps, me, pre, bias_end(z, me), start_of, save, gated_v, fa_v, fb_v, out_v, total
            )
        for group in saves.values():
            for copy in group:
                copy.wait()
        if count == 1:
            mask_in.wait()
            for copy in x_taps:
                copy.wait()

    outs, out_specs = [], []
    for _ in range(count):
        outs += [kept(z.res, z.frames), kept(z.frames, z.res), kept(z.frames, z.res), kept(z.res, z.frames)]
        out_specs += [whole(ANY)] * 4
    outs.append(jax.ShapeDtypeStruct((z.group, z.frames), F32))
    out_specs.append(whole())
    return call(
        body,
        "forward_group",
        tuple(outs),
        [
            pltpu.VMEM((2, z.gate, z.all_rows), BF),
            pltpu.VMEM((z.gate, z.x_rows), BF),
            pltpu.VMEM((2, z.all_rows, z.frames), BF),
            pltpu.VMEM((z.x_rows, z.frames), BF),
            pltpu.VMEM((2, z.me_rows, z.res), BF),
            pltpu.VMEM((2, z.gate, width), F32),
            pltpu.VMEM((2, z.res, z.frames), BF),
            pltpu.VMEM((2, z.frames, z.res), BF),
            pltpu.VMEM((2, z.frames, z.res), BF),
            pltpu.VMEM((z.cycle, 32, z.frames), BF),
            pltpu.SemaphoreType.DMA((8 + count * (4 * parts + 3),)),
        ],
        in_specs=[whole(ANY)] * (n_sources + n_packs + 2) + [whole()],
        out_specs=tuple(out_specs),
        flops=8 * count * z.frames * z.gate * z.taps,
        nbytes=40 * MIB,
        vmem=50,
    )


def gradient_group(z, high, n_after, n_high, n_low, n_packs):
    low = high - 1
    last, first = high == z.cycle - 1, low == 0
    width = 256
    shares = z.blocks // 2
    half_rows = z.share_rows // 2
    extra = z.share_first // 2 if first else 0

    def body(s_ref, *refs):
        refs = list(refs)
        take = lambda n: [refs.pop(0) for _ in range(n)]
        take(n_after)
        sources = {high: take(n_high), low: take(n_low)}
        packs = take(n_packs)
        (x_ref, mask_ref, end_ref, stream_high) = take(4)
        if last:
            (res_ref, zcot_ref, cot_det_ref, mixed_ref, endb_ref, lu_ref) = take(6)
            other_gated = take(z.cycle - 2)
        else:
            (dres_in, h_in, dx_in) = take(3)
            saved_high = take(3)
        saved_low = take(3)
        if first:
            (turned_in, sx_ref, base_ref, matrix_ref, audio_ref, lu_ref, det_ref) = take(7)
        else:
            (stream_low, turned_in) = take(2)
        (stay_ref, cross_ref) = take(2)
        if first:
            (tail_ref, mel_ref, agrad_ref) = take(3)
        else:
            (h_out, dx_out) = take(2)
        if last:
            (p_ref, a_ref, latent_ref, logdet_ref, dres_out, base_out) = take(6)
        (wides, mes, all_taps, gated_vs, fa_vs, fb_vs, dpre, grads, hs, dx_ref, turned, dres_ref, masks, sems) = take(14)
        if last:
            (pre, total, spare) = take(3)
        if first:
            (low_wide, low_grads, in_v) = take(3)
        copies = Copies(sems)

        mask_in = copies.start(mask_ref, masks)
        high_in = [copies.start(stream_high, all_taps.at[0, pl.ds(z.res, z.res)])]
        if not last:
            gate_in = [copies.start(dres_in, dres_ref)]
        pack_high, taps_high = copies.weights(
            z, s_ref, sources[high], packs, high, wides.at[0], mes.at[0], z.taps
        )
        x_in = [copies.start(x_ref, all_taps.at[0, pl.ds(z.taps, z.x_rows)])]
        if not last:
            gate_in += [copies.start(h_in, hs.at[0])]
            gate_in += [copies.start(a, b.at[0]) for a, b in zip(saved_high[1:], (fa_vs, fb_vs))]
            mix_in = [copies.start(saved_high[0], gated_vs.at[0]), copies.start(dx_in, dx_ref)]
        else:
            mix_in = [copies.start(a, spare.at[i]) for i, a in enumerate(other_gated[:2])]
        turned_copy = copies.start(turned_in, turned)
        low_k = 0 if first else 1
        if first:
            in_copies = taps_copies(z, s_ref, sources[0], 0, in_v, sems.at[copies.used])
            copies.used += 1
            low_x = all_taps.at[0, pl.ds(z.taps, z.x_rows)]
            pack_low, taps_low = copies.weights(z, s_ref, None, packs, 0, low_wide, mes.at[1], 0)
            each(in_copies, "start")
            low_in = []
        else:
            low_x = all_taps.at[1, pl.ds(z.taps, z.x_rows)]
            low_in = [copies.start(stream_low, all_taps.at[1, pl.ds(z.res, z.res)])]
            pack_low, taps_low = copies.weights(
                z, s_ref, sources[low], packs, low, wides.at[1], mes.at[1], z.taps
            )
            x_in.append(copies.start(x_ref, low_x))
        gate_low = [copies.start(a, b.at[1]) for a, b in zip(saved_low[1:], (fa_vs, fb_vs))]
        mix_low = copies.start(saved_low[0], gated_vs.at[1])

        for k in range(2):
            mes[k, z.pack_cond :, :] = jnp.zeros((z.me_rows - z.pack_cond, z.res), BF)
        mask_in.wait()
        for copy in high_in:
            copy.wait()
        fill_taps(z, all_taps.at[0], masks.at[high], high)
        for copy in x_in:
            copy.wait()
        each(pack_high, "wait")
        if last:
            each(taps_high, "wait")
            lu = lu_ref[...]
            r = lax.broadcasted_iota(jnp.int32, lu.shape, 0)
            c = lax.broadcasted_iota(jnp.int32, lu.shape, 1)
            trace = jnp.sum(jnp.where(r == c, lu, 0.0))
            total[...] = res_ref[...]
            forward_parts(
                z, high, wides.at[0], all_taps.at[0], mes.at[0], pre, bias_end(z, mes.at[0]) + endb_ref[...],
                None, lambda part: None, gated_vs.at[0], fa_vs.at[0], fb_vs.at[0], None, total,
            )
            h = z.half
            is_scale = lax.broadcasted_iota(jnp.int32, (z.group, z.frames), 0) < h
            turn = lambda rows: pltpu.roll(rows, h, axis=0)
            ends = total[...]
            growth = jnp.where(is_scale, jnp.exp(jnp.where(is_scale, ends, 0.0)), 0.0)
            mixed, zcot = mixed_ref[...], zcot_ref[...]
            grown = growth * turn(mixed)
            latent_ref[...] = jnp.where(is_scale, mixed, turn(grown) + ends)
            logdet_ref[...] = jnp.sum(jnp.where(is_scale, ends, 0.0), axis=0, keepdims=True) + trace
            dres = jnp.where(is_scale, turn(zcot) * grown + cot_det_ref[...], zcot)
            dres = jnp.concatenate([dres, dres, jnp.zeros((LANES - 16, z.frames), F32)], axis=0)
            dres_ref[...] = dres.T.astype(BF)
            base_out[...] = zcot * jnp.where(is_scale, 1.0, turn(growth))
            leaving = [copies.start(dres_ref, dres_out)]
        else:
            for copy in gate_in:
                copy.wait()
            leaving = []

        two = lambda exact: jnp.concatenate(
            [exact.astype(BF).astype(F32), exact - exact.astype(BF).astype(F32)], axis=0
        ).astype(BF)
        dsum = jnp.sum(dres_ref[...].astype(F32), axis=0, keepdims=True)
        end_bias = mm(two(jnp.concatenate([dsum, jnp.zeros((7, LANES), F32)], axis=0)), end_ref[16:, :])
        end_bias = end_bias[0:8] + end_bias[8:16]

        def gate_and_mix(layer, k, h_ref, grad_rows, at, ready):
            me = mes.at[k]
            for n in range(z.res // width):
                cols = slice(n * width, (n + 1) * width)
                dgated = mm(dres_ref[...], me[z.res :, cols])
                if h_ref is not None:
                    dgated = dgated + mm(h_ref[...], me[0 : z.res, cols])
                dpre[:, cols] = (dgated * fa_vs[k, :, cols].astype(F32)).astype(BF)
                dpre[:, z.res + n * width : z.res + (n + 1) * width] = (
                    dgated * fb_vs[k, :, cols].astype(F32)
                ).astype(BF)
            for copy in ready:
                copy.wait()
            outer = mm(gated_vs[k], dres_ref[...]).T[0 : z.group]
            mix_grad = mm(end_ref[0:16, :], two(outer), 0, 0)
            bias_grad = end_bias
            if h_ref is not None:
                h_mix = mm(gated_vs[k], h_ref[...]).T
                mix_grad = mix_grad + jnp.concatenate([h_mix, jnp.zeros((z.skip, z.res), F32)], axis=0)
                h_sum = jnp.sum(h_ref[...].astype(F32), axis=0, keepdims=True)
                h_sum = jnp.concatenate([h_sum, jnp.zeros((7, z.res), F32)], axis=0)
                bias_grad = bias_grad + jnp.concatenate([h_sum, jnp.zeros((8, z.skip), F32)], axis=1)
            mix_grad = mix_grad.astype(BF)
            for s in range(z.blocks):
                for j in range(z.m_fold):
                    top = at + j * z.m_rows
                    grad_rows[s, top : top + z.m_rows, :] = mix_grad[
                        s * z.m_rows : (s + 1) * z.m_rows, j * LANES : (j + 1) * LANES
                    ]
            return outer, bias_grad

        row = lax.broadcasted_iota(jnp.int32, (z.x_rows, LANES), 0)

        def with_bias(block, bias_grad, s):
            moved = pltpu.roll(bias_grad, (z.mixed_rows - s * z.m_rows) % z.mixed_rows, axis=1) if s else bias_grad
            return jnp.where(row == z.x_rows - 1, moved[0:1, 0:LANES], block).astype(BF)

        def taps_gradients(k, bias_grad):
            for n in range(z.gate // width):
                part = mm(all_taps[k], dpre[:, n * width : (n + 1) * width])
                for i in range(width // LANES):
                    s = n * (width // LANES) + i
                    lanes = slice(i * LANES, (i + 1) * LANES)
                    grads[s, 0 : z.taps, :] = part[0 : z.taps, lanes].astype(BF)
                    grads[s, z.taps : z.taps + z.x_rows, :] = with_bias(part[z.taps :, lanes], bias_grad, s)

        sent_sem = sems.at[copies.used]
        copies.used += 1

        def send(layer, grad_rows, rows, top):
            owner = max(layer, 1)
            away = (s_ref[0] ^ owner) & 1
            off_side = ((s_ref[0] ^ owner) >> 1) & 1
            for s in range(z.blocks):
                for half in range(2):
                    if z.direct:
                        v = s_ref[1] ^ s
                        place = (off_side ^ half) << (z.bits - 1)
                        for b in range(1, z.bits):
                            place = place | (((v >> b) & 1) << (z.bits - 1 - b))
                        to_stay = (v & 1) == away
                        role = away
                    else:
                        place, to_stay = jnp.int32((s % shares) * 2 + half), jnp.int32(s) < shares
                        role = jnp.int32(high - layer)
                    block = grad_rows.at[s, pl.ds(half * rows, rows)]
                    if first:
                        stay_at = stay_ref.at[place, pl.ds(top, rows)]
                        cross_at = cross_ref.at[place, pl.ds(top, rows)]
                    else:
                        stay_at = stay_ref.at[role, place]
                        cross_at = cross_ref.at[1 - role if z.direct else role, place]

                    @pl.when(to_stay)
                    def _():
                        pltpu.make_async_copy(block, stay_at, sent_sem).start()

                    @pl.when(jnp.logical_not(to_stay))
                    def _():
                        pltpu.make_async_copy(block, cross_at, sent_sem).start()

        def sent_wait(grad_rows, rows):
            target = stay_ref.at[0, pl.ds(0, rows)] if first else stay_ref.at[0, 0]
            for _ in range(2 * z.blocks):
                pltpu.make_async_copy(grad_rows.at[0, pl.ds(0, rows)], target, sent_sem).wait()

        def stream_gradient(layer, k, h_ref, new_h):
            d = 2**layer
            dx = mm(dpre[...], wides[k, :, z.taps :])
            dx_ref[...] = dx if layer == z.cycle - 1 else dx + dx_ref[...]
            keep_before = turned[:, 2 * layer : 2 * layer + 1]
            keep_after = turned[:, 2 * layer + 1 : 2 * layer + 2]
            for n in range(z.res // width):
                cols = slice(n * width, (n + 1) * width)
                side = [
                    mm(dpre[...], wides[k, :, i * z.res + n * width : i * z.res + (n + 1) * width]) for i in range(3)
                ]
                result = side[1] + pltpu.roll(side[0] * keep_before, z.frames - d, axis=0)
                result = result + pltpu.roll(side[2] * keep_after, d, axis=0)
                if h_ref is not None:
                    result = result + h_ref[:, cols].astype(F32)
                new_h[:, cols] = result.astype(BF)

        h_high = None if last else hs.at[0]
        outer, bias_grad = gate_and_mix(high, 0, h_high, grads, z.taps + z.x_rows, [] if last else mix_in)
        if last:
            p_ref[high, :, :] = outer
            a_ref[...] = mm(all_taps[0, z.taps :, :], dres_ref[...]).T[0 : z.group]
            for i in range(z.cycle - 2):
                mix_in[i].wait()
                p_ref[i, :, :] = mm(spare[i % 2], dres_ref[...]).T[0 : z.group]
                if i + 2 < z.cycle - 2:
                    mix_in.append(copies.start(other_gated[i + 2], spare.at[i % 2]))
        taps_gradients(0, bias_grad)
        send(high, grads, half_rows, 0)
        turned_copy.wait()
        if not last:
            each(taps_high, "wait")
        stream_gradient(high, 0, h_high, hs.at[1])
        for copy in low_in:
            copy.wait()
        if not first:
            fill_taps(z, all_taps.at[1], masks.at[low], low)
        each(pack_low, "wait")
        for copy in gate_low:
            copy.wait()
        sent_wait(grads, half_rows)
        if not first:
            outer, bias_grad = gate_and_mix(low, 1, hs.at[1], grads, z.taps + z.x_rows, [mix_low])
            if last:
                p_ref[low, :, :] = outer
            taps_gradients(1, bias_grad)
            send(low, grads, half_rows, 0)
            each(taps_low, "wait")
            stream_gradient(low, 1, hs.at[1], hs.at[0])
            leaving += [copies.start(hs.at[0], h_out), copies.start(dx_ref, dx_out)]
            sent_wait(grads, half_rows)
        else:
            outer, bias_grad = gate_and_mix(0, 1, hs.at[1], low_grads, z.x_rows, [mix_low])
            dcond = mm(low_x[...], dpre[...])
            for s in range(z.blocks):
                low_grads[s, 0 : z.x_rows, :] = with_bias(dcond[:, s * LANES : (s + 1) * LANES], bias_grad, s)
            send(0, low_grads, extra, half_rows)
            h = z.half
            g_first = hs.at[0]
            g_first[...] = (hs[1].astype(F32) + mm(dres_ref[...], end_ref[16:, 0 : z.res])).astype(BF)
            dx = dx_ref[...] + mm(dpre[...], low_wide[...]) + mm(g_first[...], sx_ref[0 : z.res, :])
            dx = dx.T
            hx = mm(low_x[...], g_first[...])

            def folded(rows, tap):
                base = z.tap(tap)
                return [rows[base : base + h] + rows[base + h : base + 2 * h], rows[base + 3 * h : base + 3 * h + 1]]

            q = jnp.concatenate(
                folded(dcond, 0) + folded(dcond, 1) + folded(dcond, 2) + [jnp.zeros((16 - 3 * (h + 1), z.gate), F32)],
                axis=0,
            )
            each(in_copies, "wait")
            back = mm(two(q), in_v[...])
            start_rows = jnp.concatenate(folded(hx, 1), axis=0)
            for tap in range(3):
                top = tap * (h + 1)
                part = back[:, tap * z.res : (tap + 1) * z.res]
                start_rows = start_rows + part[top : top + h + 1] + part[16 + top : 16 + top + h + 1]
            tail_ref[...] = jnp.zeros_like(tail_ref)
            tail_ref[0 : h + 1, :] = start_rows
            mel_ref[...] = dx[0 : z.mel, :]
            keep_before = masks[0, 0:16, :].astype(F32)[0:h]
            keep_after = masks[0, 16:32, :].astype(F32)[0:h]
            tap_rows = []
            for tap in range(3):
                base = z.tap(tap)
                tap_rows.append(dx[base : base + h, :] + dx[base + 2 * h : base + 3 * h, :])
            zero = jnp.zeros((8 - h, z.frames), F32)
            pad = lambda v: jnp.concatenate([v, zero], axis=0)
            front = pad(tap_rows[1])
            front = front + pltpu.roll(pad(tap_rows[0] * keep_before), z.frames - 1, axis=1)
            front = front + pltpu.roll(pad(tap_rows[2] * keep_after), 1, axis=1)
            dmixed = front + base_ref[...]
            matrix = matrix_ref[...]
            r = lax.broadcasted_iota(jnp.int32, matrix.shape, 0)
            c = lax.broadcasted_iota(jnp.int32, matrix.shape, 1)
            flipped = matrix.T
            agrad = jnp.zeros((z.group, z.frames), F32)
            for k in range(z.group):
                agrad = agrad + flipped[:, k : k + 1] * dmixed[k : k + 1, :]
            agrad_ref[...] = agrad
            dmatrix = jnp.zeros((z.group, z.group), F32)
            for k in range(z.group):
                column = jnp.sum(dmixed * audio_ref[k : k + 1, :], axis=1, keepdims=True)
                dmatrix = dmatrix + jnp.where(c == k, column, 0.0)
            lu = lu_ref[...]
            lower = jnp.where(r > c, lu, 0.0) + jnp.where(r == c, 1.0, 0.0)
            grown = jnp.where(r == c, jnp.exp(lu), 0.0)
            upper = jnp.where(r < c, lu, 0.0) + grown
            upper_t = upper.T
            lower_t = lower.T
            dlower = jnp.zeros_like(lu)
            dupper = jnp.zeros_like(lu)
            for k in range(z.group):
                dlower = dlower + dmatrix[:, k : k + 1] * upper_t[k : k + 1, :]
                dupper = dupper + lower_t[:, k : k + 1] * dmatrix[k : k + 1, :]
            total_lu = jnp.where(r > c, dlower, 0.0) + jnp.where(r < c, dupper, 0.0) + dupper * grown
            tail_ref[8 : 8 + z.group, 0 : z.group] = total_lu + jnp.where(r == c, jnp.sum(det_ref[...]), 0.0)
            tail_ref[8:9, LANES : 2 * LANES] = dsum
            sent_wait(low_grads, extra)
        for copy in leaving:
            copy.wait()

    def column(rows):
        return pl.BlockSpec((rows, z.frames), lambda i, s: (0, s[2]))

    in_specs = [whole(ANY)] * (n_after + n_high + n_low + n_packs + 2) + [whole(), whole(ANY)]
    if last:
        in_specs += [whole(), column(z.group), column(1), whole(), whole(), whole()] + [whole(ANY)] * (z.cycle - 2)
    else:
        in_specs += [whole(ANY)] * 6
    in_specs += [whole(ANY)] * 3
    if first:
        in_specs += [whole(ANY), whole(), whole(), whole(), column(z.group), whole(), column(1)]
    else:
        in_specs += [whole(ANY)] * 2
    lead = () if first else (2,)
    outs = [pltpu.HBM((*lead, 2 * shares, half_rows + extra, LANES), BF)] * 2
    out_specs = [whole(ANY)] * 2
    if first:
        outs += [
            jax.ShapeDtypeStruct((16, z.res), F32),
            jax.ShapeDtypeStruct((z.mel, z.frames), F32),
            jax.ShapeDtypeStruct((z.group, z.frames), F32),
        ]
        out_specs += [whole()] * 3
    else:
        outs += [kept(z.frames, z.res), kept(z.frames, z.x_rows, F32)]
        out_specs += [whole(ANY)] * 2
    if last:
        outs += [
            jax.ShapeDtypeStruct((z.cycle, z.group, z.res), F32),
            jax.ShapeDtypeStruct((z.group, z.x_rows), F32),
            jax.ShapeDtypeStruct((z.group, z.frames), F32),
            jax.ShapeDtypeStruct((1, z.frames), F32),
            kept(z.frames, LANES),
            jax.ShapeDtypeStruct((z.group, z.frames), F32),
        ]
        out_specs += [whole()] * 4 + [whole(ANY), whole()]
    sets = 1 if first else 2
    scratch = [
        pltpu.VMEM((sets, z.gate, z.all_rows), BF),
        pltpu.VMEM((2, z.me_rows, z.res), BF),
        pltpu.VMEM((sets, z.all_rows, z.frames), BF),
        pltpu.VMEM((2, z.res, z.frames), BF),
        pltpu.VMEM((2, z.frames, z.res), BF),
        pltpu.VMEM((2, z.frames, z.res), BF),
        pltpu.VMEM((z.frames, z.gate), BF),
        pltpu.VMEM((z.blocks, z.share_rows, LANES), BF),
        pltpu.VMEM((2, z.frames, z.res), BF),
        pltpu.VMEM((z.frames, z.x_rows), F32),
        pltpu.VMEM((z.frames, z.x_rows), F32),
        pltpu.VMEM((z.frames, LANES), BF),
        pltpu.VMEM((z.cycle, 32, z.frames), BF),
        pltpu.SemaphoreType.DMA((40,)),
    ]
    if last:
        scratch += [
            pltpu.VMEM((2, z.gate, width), F32),
            pltpu.VMEM((z.group, z.frames), F32),
            pltpu.VMEM((2, z.res, z.frames), BF),
        ]
    if first:
        scratch += [
            pltpu.VMEM((z.gate, z.x_rows), BF),
            pltpu.VMEM((z.blocks, z.share_first, LANES), BF),
            pltpu.VMEM((z.gate, z.taps), BF),
        ]
    return call(
        body,
        "gradient_first" if first else "gradient_last" if last else "gradient_group",
        tuple(outs),
        scratch,
        in_specs=in_specs,
        out_specs=tuple(out_specs),
        flops=(60 if last else 40) * z.frames * z.gate * z.taps,
        nbytes=20 * MIB,
        vmem=58,
    )


def finish(z):
    def body(s_ref, own_ref, mix_ref, mb_ref, st_ref, a_ref, out_ref):
        h = z.half
        outer = own_ref[0 : z.group, :]
        high = outer.astype(BF).astype(F32)
        ends = mm(jnp.concatenate([high, outer - high], axis=0).astype(BF), mix_ref[...], 1, 1)
        ends = ends[0 : z.group] + ends[z.group :] + own_ref[8 : 8 + z.group, 0:1] * mb_ref[...]
        base = z.tap(1)
        a = a_ref[...]
        front = jnp.zeros((z.group, z.res), F32)
        for j in range(h + 1):
            if j < h:
                column = a[:, base + j : base + j + 1] + a[:, base + h + j : base + h + j + 1]
            else:
                column = a[:, base + 3 * h : base + 3 * h + 1]
            front = front + column * st_ref[j : j + 1, :]
        out_ref[0:8, :] = ends[:, 0 : z.res] + front
        out_ref[8:16, :] = jnp.zeros((8, z.res), F32)
        out_ref[8:16, 0 : z.skip] = ends[:, z.res :]

    return call(
        body,
        "finish",
        jax.ShapeDtypeStruct((16, z.res), F32),
        [],
        in_specs=[whole()] * 5,
        out_specs=whole(),
        flops=1e7,
        nbytes=MIB,
    )


def permute(z, block, move):
    pairs = []
    for dp in range(z.data):
        for li in range(z.cycle):
            to = move(dp, li)
            if to is not None:
                pairs.append((dp * z.cycle + li, to[0] * z.cycle + to[1]))
    return lax.ppermute(block, ("dp", "layer"), pairs)


def in_hbm(arrays):
    return [pltpu.with_memory_space_constraint(array, pltpu.HBM) for array in arrays]


def tie(value, *earlier):
    return lax.optimization_barrier((value, *earlier))[0]


def near_weights(z, in_w, group_place, prepared):
    if z.cycle != 4:
        ready = prepared()
        gathered = lax.all_gather(in_w, "layer")
        return ready, layer_packs(z, ready[0]), [gathered], gathered
    rows = z.gate // 2
    part = lax.dynamic_slice_in_dim(in_w, (group_place & 1) * rows, rows, 0)
    far = permute(z, part, lambda dp, li: (dp, li ^ 2) if li in (1, 2) else None)
    near = permute(z, in_w, lambda dp, li: (dp, li ^ 1))
    ready = prepared()
    packs = layer_packs(z, ready[0])
    far = tie(far, ready[1], packs[1])
    beside = permute(z, far, lambda dp, li: (dp ^ 1, li) if li in (3, 0) else None)
    far_late = permute(z, tie(in_w, far, packs[2]), lambda dp, li: (dp, li ^ 2) if li in (3, 0) else None)
    across = lambda dp, li: (dp, li ^ 1) if li in (3, 0) else None
    cross, cross_beside = permute(z, far, across), permute(z, beside, across)
    return ready, packs, [in_w, near, far, beside, cross, cross_beside], far_late


def late_weights(z, sources, far, token):
    if z.cycle != 4:
        return sources
    far = tie(far, token)
    return [*sources[:2], far, permute(z, far, lambda dp, li: (dp, li ^ 1) if li in (1, 2) else None)]


def layer_packs(z, pack):
    if z.cycle != 4:
        return [lax.all_gather(pack, "layer")]
    near = permute(z, pack, lambda dp, li: (dp, li ^ 1))
    far = permute(z, pack, lambda dp, li: (dp, li ^ 2))
    cross = permute(z, far, lambda dp, li: (dp, li ^ 1))
    return [pack, near, far, cross]


def add(*terms):
    total = terms[0].astype(F32)
    for term in terms[1:]:
        total = total + term.astype(F32)
    return total


def sent(z, blocks, *moves):
    many = isinstance(blocks, list)
    blocks = blocks if many else [blocks]
    got = yield blocks, [permute(z, block, move) for block, move in zip(blocks, moves)]
    return got if many else got[0]


def meet_core(z, stay, cross):
    got = yield from sent(z, cross, lambda dp, li: (dp, li ^ 1))
    count = z.data // 2
    if stay.ndim == 3:
        stay, got = stay[None], got[None]
    near = [add(stay[role, :count], got[role, :count]).astype(BF) for role in range(stay.shape[0])]
    far = [add(stay[role, count:], got[role, count:]).astype(BF) for role in range(stay.shape[0])]
    return near, far


def reduce_chips(z, side, at_home, operands):
    near, far, near_other, far_other = operands
    count = z.data // 2
    away = (lambda li: not at_home(li)) if near is near_other else at_home
    by_y, by_x, by_both = yield from sent(
        z,
        [far, near_other, far_other],
        lambda dp, li: (dp, li ^ 2) if at_home(li) else None,
        lambda dp, li: (dp ^ 1, li ^ 1) if away(li) else None,
        lambda dp, li: (dp ^ 1, li ^ 3) if away(li) else None,
    )
    parts = [near, by_y, by_x, by_both]
    for b in range(1, z.bits):
        count //= 2
        send = add(*(part[count:] for part in parts)).astype(BF)
        keep = add(*(part[:count] for part in parts)).astype(BF)
        got = yield from sent(z, send, lambda dp, li: (dp ^ (1 << b), li) if at_home(li) else None)
        parts = [keep, got]
    total = add(keep[0], got[0])
    got = yield from sent(
        z, total.astype(BF), lambda dp, li: (dp, li ^ 2) if at_home(li) and (li & 2) != side else None
    )
    return total, got.astype(F32)


def reduce_last_two(z, stay, cross):
    near, far = yield from meet_core(z, stay, cross)
    operands = (near[0], far[0], near[1], far[1])
    total, got = yield from reduce_chips(z, 2, lambda li: True, operands)
    return jnp.concatenate([total, got], axis=0)


def reduce_first_two(z, stay, cross):
    near, far = yield from meet_core(z, stay, cross)
    operands = (near[0], far[0], near[0], far[0])
    total, got = yield from reduce_chips(z, 0, lambda li: (li & 1) == 1, operands)
    cut = z.share_rows // 2
    share = jnp.concatenate([total[cut:], got[cut:]], axis=0)
    share = yield from sent(z, share.astype(BF), lambda dp, li: (dp, 0) if li == 1 else None)
    return share.astype(F32), jnp.concatenate([total[:cut], got[:cut]], axis=0)


def sum_of_own_layer(z, stacked, place):
    bit = 0
    while (1 << bit) < z.cycle:
        mine = (place >> bit) & 1
        pairs = stacked.reshape((stacked.shape[0] // 2, 2) + stacked.shape[1:])
        own = lax.dynamic_index_in_dim(pairs, mine, 1, keepdims=False)
        other = lax.dynamic_index_in_dim(pairs, 1 - mine, 1, keepdims=False)
        got = yield from sent(z, other, lambda dp, li: (dp, li ^ (1 << bit)))
        stacked = own + got
        bit += 1
    return stacked[0]


class Chain:
    def __init__(self, steps):
        self.steps, self.result = steps, None
        self.leaving, self.arriving = next(steps)

    def go_on(self, arrived):
        try:
            self.leaving, self.arriving = self.steps.send(arrived)
        except StopIteration as end:
            self.leaving, self.arriving, self.result = [], [], end.value


def advance(chains, *tokens):
    chains = [chain for chain in chains if chain.arriving]
    if not chains:
        return []
    sizes = [len(chain.arriving) for chain in chains]
    arrived = list(lax.optimization_barrier((*sum((chain.arriving for chain in chains), []), *tokens)))
    marks = [arrived[0]]
    for chain, size in zip(chains, sizes):
        chain.go_on(arrived[:size])
        arrived = arrived[size:]
    return marks


def reduce_whole(z, stay, cross):
    rows = jnp.concatenate([stay, cross], axis=0)
    rows = rows.reshape(z.blocks, 2 * rows.shape[1], LANES)
    at = rows.shape[1] - z.share_first
    mix = rows[:, at + z.x_rows :].reshape(z.blocks, z.m_fold, z.m_rows, LANES)
    mix = mix.transpose(0, 2, 1, 3).reshape(z.mixed_rows, z.res)
    bias = rows[:, at + z.x_rows - 1, : z.m_rows].reshape(z.mixed_rows)
    wide = rows[:, : at + z.x_rows].transpose(0, 2, 1).reshape(z.gate, at + z.x_rows)
    out = []
    for part in (wide, mix, bias):
        part = lax.psum(part.astype(F32), "layer").astype(BF)
        out.append(lax.psum_scatter(part, "dp", scatter_dimension=0, tiled=True).astype(F32))
    return tuple(out)


def sum_of_all(z, values):
    moves = [(0, 1)]
    moves += [(1 << b, 0) for b in range(1, z.data.bit_length() - 1)] + [(1, 0)]
    moves += [(0, 1 << b) for b in range(1, z.cycle.bit_length() - 1)]
    for a, b in moves:
        values = values + (yield from sent(z, values, lambda dp, li: (dp ^ a, li ^ b)))
    return values


def per_device(*args):
    (
        audio_in,
        mel_spec,
        lengths,
        z_cotangent,
        det_cotangent,
        lu_weight,
        start_weight,
        start_bias,
        in_weight,
        cond_weight,
        gate_bias,
        mix_weight,
        mix_bias,
        end_weight,
        end_bias,
    ) = args
    cycle, data = lax.axis_size("layer"), lax.axis_size("dp")
    z = Sizes(args, cycle, data)
    place, group_place = lax.axis_index("layer"), lax.axis_index("dp")
    scalars = jnp.stack([place, group_place, place // z.copies]).astype(jnp.int32)
    in_w, mix = in_weight[0], mix_weight[0]
    start_rows = jnp.concatenate([start_weight.T, start_bias[None], jnp.zeros((7 - z.half, z.res), F32)], axis=0)
    det_row = det_cotangent[None, :]
    ends = jnp.concatenate([end_weight, end_weight, end_weight, jnp.zeros((LANES - z.group, z.mixed_rows), BF)], axis=0)

    def prepared():
        pack, start_x = prepare_weights(z, in_w, cond_weight, gate_bias, mix, mix_bias, start_rows, end_weight)(
            scalars, in_w, cond_weight[0], gate_bias, mix, mix_bias, start_rows, end_weight
        )
        x, mixed, masks, turned, matrix = prepare_frames(z)(scalars, lengths, audio_in, mel_spec, lu_weight)
        return pack, x, start_x, mixed, masks, turned, matrix

    (_, x, start_x, mixed, masks, turned, matrix), packs, early, far_late = near_weights(
        z, in_w, group_place, prepared
    )

    packs, (x, masks, turned) = in_hbm(packs), in_hbm((x, masks, turned))
    *saved, totals = forward_group(z, len(early), len(packs))(scalars, *early, *packs, x, masks, start_x)
    saved = [in_hbm(saved[4 * layer : 4 * layer + 4]) for layer in range(cycle - 1)]
    late = late_weights(z, early, far_late, totals)

    own = None
    if z.copies > 1:
        own = ((place % z.copies) == 0).astype(F32)
    mine = lambda v: v if own is None else (v * own.astype(v.dtype))
    blocks, after = {}, []
    for high in range(cycle - 1, 0, -2):
        low = high - 1
        if z.direct and not low:
            while own_outer.result is None:
                advance([own_outer])
            advance([pair], own_outer.result)
            after = [*pair.leaving]
        at_high = late if high == cycle - 1 else early
        at_low = late if low == 0 else early
        kernel = gradient_group(z, high, len(after), len(at_high), len(at_low), len(packs))
        ins = [*after, *at_high, *at_low, *packs, x, masks, ends, saved[low][3]]
        if high == cycle - 1:
            ins += [totals, z_cotangent, det_row, mixed, end_bias[:, None], lu_weight]
            ins += [saved[other][0] for other in range(cycle - 2)]
        else:
            ins += in_hbm([dres, h, dx]) + saved[high][:3]
        ins += saved[low][:3]
        if low:
            ins += [saved[low - 1][3], turned]
        else:
            ins += [turned, start_x, base, matrix, audio_in, lu_weight, det_row]
        stay, cross, *outs = kernel(scalars, *ins)
        blocks[high] = (mine(stay), mine(cross))
        if low:
            h, dx, *outs = outs
        else:
            tail, mel_grad, audio_grad = outs
        if high == cycle - 1:
            outer, a_part, latent, logdet, dres, base = outs
            dsum_rows = jnp.broadcast_to(a_part[:, z.ones : z.ones + 1], (cycle, z.group, z.res))
            own_outer = Chain(sum_of_own_layer(z, mine(jnp.concatenate([outer, dsum_rows], axis=1)), place))
            if z.direct:
                pair = Chain(reduce_last_two(z, *blocks[high]))

    if z.direct:
        token = advance([pair], tail)
        tail = tie(tail, *token)
        blocks[1] = [tie(block, *token) for block in blocks[1]]
    else:
        token = []
        while own_outer.result is None:
            token = advance([own_outer], *token)
    end_part = finish(z)(scalars, own_outer.result, mix, mix_bias, start_rows, mine(a_part))
    small = Chain(sum_of_all(z, jnp.concatenate([end_part, mine(tail)], axis=0)))
    active = [small]
    if z.direct:
        both = Chain(reduce_first_two(z, *blocks[1]))
        active += [both, pair]
    while any(chain.arriving for chain in active):
        token = advance(active, *token)
    whole_sum = small.result
    end_weight_grad = jnp.concatenate([whole_sum[0:8], whole_sum[8:16, : z.skip]], axis=1)
    lu_grad = whole_sum[24:32, : z.group]
    end_bias_grad = whole_sum[24, LANES : LANES + z.group]
    start_weight_grad = whole_sum[16 : 16 + z.half].T
    start_bias_grad = whole_sum[16 + z.half]

    if z.direct:
        first_share, share = both.result
        share = jnp.where(place >= 2, pair.result, share)
        short = jnp.where(place == 0, first_share, share[z.taps :])
        conds = short[: z.x_rows].T
        mix_grad = short[z.x_rows :].reshape(z.m_fold, z.m_rows, LANES)
        mix_grad = jnp.concatenate([mix_grad[j] for j in range(z.m_fold)], axis=1)
        mix_bias_grad = short[z.x_rows - 1, : z.m_rows]
        in_grad = share[: z.taps].T
    else:
        wide = mix_grad = mix_bias_grad = None
        for layer in range(cycle):
            high = layer + (layer + 1) % 2
            rows = z.share_rows // 2
            stay, cross = blocks[high]
            if high > 1:
                stay, cross = stay[high - layer], cross[high - layer]
            elif layer:
                stay, cross = stay[:, :rows], cross[:, :rows]
            else:
                stay, cross = stay[:, rows:], cross[:, rows:]
            new = reduce_whole(z, stay, cross)
            if not layer:
                wide, mix_grad, mix_bias_grad = (jnp.pad(new[0], ((0, 0), (z.taps, 0))), *new[1:])
                continue
            wide, mix_grad, mix_bias_grad = jax.tree.map(
                lambda now, old: jnp.where(place == layer, now, old), new, (wide, mix_grad, mix_bias_grad)
            )
        in_grad, conds = wide[:, : z.taps], wide[:, z.taps :]
    rows = conds[:, z.first : z.first + 3 * z.tap_rows].reshape(-1, 3, z.tap_rows)
    half = z.half
    rows = jnp.concatenate([rows[:, :, :half] + rows[:, :, half : 2 * half], rows[:, :, 3 * half : 3 * half + 1]], 2)
    first_in_grad = jnp.einsum("rkj,jc->rkc", rows, start_rows[: half + 1], precision=highest).reshape(-1, z.taps)
    in_grad = jnp.where(place == 0, first_in_grad, in_grad)

    def own_columns(rows):
        if z.copies == 1:
            return rows
        width = z.frames // z.copies
        return lax.dynamic_slice_in_dim(rows, (place % z.copies) * width, width, 1)

    return (
        own_columns(latent),
        own_columns(logdet)[0],
        own_columns(audio_grad),
        own_columns(mel_grad),
        lu_grad,
        start_weight_grad,
        start_bias_grad,
        in_grad[None],
        conds[None, :, : z.mel],
        conds[None, :, z.ones],
        mix_grad[None],
        mix_bias_grad[None],
        end_weight_grad,
        end_bias_grad,
    )


def solution(mesh):
    in_specs = (
        P(None, "dp"),
        P(None, "dp"),
        P("dp", None),
        P(None, "dp"),
        P("dp"),
        P(),
        P(),
        P(),
        P("layer", None, None),
        P("layer", None, None),
        P("layer", None),
        P("layer", None, None),
        P("layer", None),
        P(),
        P(),
    )
    out_specs = (
        P(None, ("dp", "layer")),
        P(("dp", "layer")),
        P(None, ("dp", "layer")),
        P(None, ("dp", "layer")),
        P(),
        P(),
        P(),
        P("layer", "dp", None),
        P("layer", "dp", None),
        P("layer", "dp"),
        P("layer", "dp", None),
        P("layer", "dp"),
        P(),
        P(),
    )
    return jax.shard_map(
        per_device, mesh=mesh, in_specs=in_specs, out_specs=out_specs, check_vma=False
    )
```

time: 1380 us -> 317 us (0.23)
  the two profiles are of different devices: /device:TPU:0 before, /device:TPU:1 now
where the time goes in v1:
time: 317 us; the launch traced here: 311 us
  Pallas kernels  116 us (37%)
  waiting for transfers between devices  110 us (35%)
  starting transfers between devices  56.2 us (18%)
  local copies, waits for them, and re-layouts  15.6 us (5%)
  other arithmetic  11.4 us (4%)
    ppermute x32, waiting for transfers between devices, permute(): return lax.ppermute(block, ('dp', 'layer'), pairs)  110 us
    pallas_call x2, Pallas kernels, per_device(): stay, cross, *outs = kernel(scalars, *ins)  85 us
    ppermute x32, starting transfers between devices, permute(): return lax.ppermute(block, ('dp', 'layer'), pairs)  56.2 us
    pallas_call x1, Pallas kernels, per_device(): forward_group(z, len(early), len(packs))  25.4 us
    unnamed x72, local copies, waits for them, and re-layouts  6.95 us
  transfers between devices with their start and end apart: 32, of which 19 were waited for; matrix products, arithmetic and copies ran while one was open for 3% of the time, Pallas kernels for 20%

profile of v1, /device:TPU:1, one launch (start us, length us, event | category | flops | bytes accessed | tf_op | source)
XLA Modules:
  0.0 311.4 jit_solution(8383930331191959988)
XLA Ops:
  0.7 2.9 dynamic-slice_bitcast_fusion
  3.6 5.2 %collective-permute-start.1 = (bf16[512,1536]{1,0:T(8,128)(2,1)}, bf16[512,1536]{1,0:T(8,128)(2,1)}, u32[]{:S(2)}, u32[]{:S(2)}) collective-permute-start(bf16[512,1536]{1,0:T(8,128)(2,1)} %dynamic-slice_bitcast_fusion), channel_id=1, source_target_pairs={{1,3},{2,0},{5,7},{6,4},{9,11},{10,8},{13,15},{14,12},{17,19},{18,... | collective-permute-start | bytes 4718600 | tf_op jit(solution)/shard_map/ppermute | solution.py:951
  14.0 2.6 prepare_frames.1
  17.3 7.9 %collective-permute-done.1.refs_2_.refs_6_.refs_5_ = bf16[512,1536]{1,0:T(8,128)(2,1)} collective-permute-done((bf16[512,1536]{1,0:T(8,128)(2,1)}, bf16[512,1536]{1,0:T(8,128)(2,1)}, u32[]{:S(2)}, u32[]{:S(2)}) %collective-permute-start.1) | collective-permute-done | bytes 1572896 | tf_op jit(solution)/shard_map/ppermute | solution.py:951
  26.0 4.3 %collective-permute-start.3 = (bf16[816,512]{1,0:T(8,128)(2,1)}, bf16[816,512]{1,0:T(8,128)(2,1)S(1)}, u32[]{:S(2)}, u32[]{:S(2)}) collective-permute-start(bf16[816,512]{1,0:T(8,128)(2,1)} %get-tuple-element.76.refs_6_.refs_10_.refs_13_), channel_id=1, source_target_pairs={{0,2},{1,3},{2,0},{3,1},{4,6},{5,7},{6,4},{7,5},{8,10},{9,11},{10,... | collective-permute-start | bytes 2506760 | tf_op jit(solution)/shard_map/ppermute | solution.py:951
  32.9 15.1 %collective-permute-done.3.refs_8_.refs_12_.refs_15_ = bf16[816,512]{1,0:T(8,128)(2,1)S(1)} collective-permute-done((bf16[816,512]{1,0:T(8,128)(2,1)}, bf16[816,512]{1,0:T(8,128)(2,1)S(1)}, u32[]{:S(2)}, u32[]{:S(2)}) %collective-permute-start.3) | collective-permute-done | bytes 835616 | tf_op jit(solution)/shard_map/ppermute | solution.py:951
  48.0 3.2 %collective-permute-start.8 = (bf16[816,512]{1,0:T(8,128)(2,1)S(1)}, bf16[816,512]{1,0:T(8,128)(2,1)S(1)}, u32[]{:S(2)}, u32[]{:S(2)}) collective-permute-start(bf16[816,512]{1,0:T(8,128)(2,1)S(1)} %collective-permute-done.3.refs_8_.refs_12_.refs_15_), channel_id=1, source_target_pairs={{0,1},{1,0},{2,3},{3,2},{4,5},{5,4},{6,7},{7,6},{8,9},{9,8},{10,11... | collective-permute-start | bytes 2506760 | tf_op jit(solution)/shard_map/ppermute | solution.py:951
  57.9 25.4 %forward_group.1 = (bf16[512,1536]{1,0:T(8,128)(2,1)}, bf16[1536,512]{1,0:T(8,128)(2,1)}, bf16[1536,512]{1,0:T(8,128)(2,1)}, bf16[512,1536]{1,0:T(8,128)(2,1)}, ...) custom-call(s32[3]{0:T(128)S(1)} %pad_add_fusion.s_ref, ...), custom_call_target="tpu_custom_call" | custom-call | flops 57982058496 | bytes 41943040 | tf_op jit(solution)/shard_map/forward_group/pallas_call | solution.py:1164
  83.4 5.9 %collective-permute-done.4.refs_2_.refs_11_ = bf16[1024,1536]{1,0:T(8,128)(2,1)} collective-permute-done((bf16[1024,1536]{1,0:T(8,128)(2,1)S(1)}, bf16[1024,1536]{1,0:T(8,128)(2,1)}, u32[]{:S(2)}, u32[]{:S(2)}) %collective-permute-start.4) | collective-permute-done | bytes 3145760 | tf_op jit(solution)/shard_map/ppermute | solution.py:951
  89.3 2.9 collective-permute-start.9
  96.2 53.8 %gradient_last.1 = (bf16[2,8,1024,128]{3,2,1,0:T(8,128)(2,1)}, bf16[2,8,1024,128]{3,2,1,0:T(8,128)(2,1)}, bf16[1536,512]{1,0:T(8,128)(2,1)}, f32[1536,128]{1,0:T...) custom-call(s32[3]{0:T(128)} %copy-done.10, ...), custom_call_target="tpu_custom_call" | custom-call | flops 144955146240 | bytes 20971520 | tf_op jit(solution)/shard_map/gradient_last/pallas_call | solution.py:1194
  152.5 4.9 %collective-permute-done.11 = f32[2,16,512]{2,1,0:T(8,128)S(1)} collective-permute-done((f32[2,16,512]{2,1,0:T(8,128)S(1)}, f32[2,16,512]{2,1,0:T(8,128)S(1)}, u32[]{:S(2)}, u32[]{:S(2)}) %collective-permute-start.11) | collective-permute-done | bytes 65568 | tf_op jit(solution)/shard_map/ppermute | solution.py:951
  160.3 4.9 %add_convert_fusion.2 = (bf16[1,4,1024,128]{3,2,1,0:T(8,128)(2,1)S(1)}, bf16[4,1024,128]{2,1,0:T(8,128)(2,1)S(1)}, bf16[4,1024,128]{2,1,0:T(8,128)(2,1)}, bf16[4,1024,128]{2,1,0:T(8,128)(2,1)}) fusion(bf16[2,8,1024,128]{3,2,1,0:T(8,128)(2,1)} %collective-permute-done.10, bf16[2,8,1024,128]{3,2,1,0:T(8,128)(2,1)} %get-tuple-element.94), kind=kLoop, calls=%fused_computation.2 | loop fusion | flops 8388608 | bytes 12582912 | tf_op jit(solution)/shard_map/convert_element_type | solution.py:1016
  169.9 31.2 %gradient_first.1 = (bf16[8,1280,128]{2,1,0:T(8,128)(2,1)}, bf16[8,1280,128]{2,1,0:T(8,128)(2,1)}, f32[16,512]{1,0:T(8,128)}, f32[80,1536]{1,0:T(8,128)}, f32[8,1536]{1,0:T(8,128)}) custom-call(s32[3]{0:T(128)} %copy-done.10, bf16[4,1024,128]{2,1,0:T(8,128)(2,1)} %get-tuple-element.171.refs_0_, bf16[4,1024,128]{2,1,0:T(8,128)(2,1)} %get-tuple-element.170.refs_1_, ...), custom_call_target="tpu_custom_call" | custom-call | flops 96636764160 | bytes 20971520 | tf_op jit(solution)/shard_map/gradient_first/pallas_call | solution.py:1194
  201.1 14.6 %collective-permute-done.15 = bf16[4,1024,128]{2,1,0:T(8,128)(2,1)S(1)} collective-permute-done((bf16[4,1024,128]{2,1,0:T(8,128)(2,1)S(1)}, bf16[4,1024,128]{2,1,0:T(8,128)(2,1)S(1)}, u32[]{:S(2)}, u32[]{:S(2)}) %collective-permute-start.15) | collective-permute-done | bytes 1048608 | tf_op jit(solution)/shard_map/ppermute | solution.py:951
  221.1 9.9 %collective-permute-done.18 = bf16[2,1024,128]{2,1,0:T(8,128)(2,1)S(1)} collective-permute-done((bf16[2,1024,128]{2,1,0:T(8,128)(2,1)S(1)}, bf16[2,1024,128]{2,1,0:T(8,128)(2,1)S(1)}, u32[]{:S(2)}, u32[]{:S(2)}) %collective-permute-start.18) | collective-permute-done | bytes 524320 | tf_op jit(solution)/shard_map/ppermute | solution.py:951
  240.6 3.3 %collective-permute-done.19 = f32[32,512]{1,0:T(8,128)S(1)} collective-permute-done((f32[32,512]{1,0:T(8,128)S(1)}, f32[32,512]{1,0:T(8,128)S(1)}, u32[]{:S(2)}, u32[]{:S(2)}) %collective-permute-start.19) | collective-permute-done | bytes 65568 | tf_op jit(solution)/shard_map/ppermute | solution.py:951
  243.9 6.7 %collective-permute-done.23 = bf16[1,1024,128]{2,1,0:T(8,128)(2,1)S(1)} collective-permute-done((bf16[1,1024,128]{2,1,0:T(8,128)(2,1)S(1)}, bf16[1,1024,128]{2,1,0:T(8,128)(2,1)S(1)}, u32[]{:S(2)}, u32[]{:S(2)}) %collective-permute-start.23) | collective-permute-done | bytes 262176 | tf_op jit(solution)/shard_map/ppermute | solution.py:951
  252.9 15.0 %collective-permute-done.22 = bf16[4,1280,128]{2,1,0:T(8,128)(2,1)S(1)} collective-permute-done((bf16[4,1280,128]{2,1,0:T(8,128)(2,1)S(1)}, bf16[4,1280,128]{2,1,0:T(8,128)(2,1)S(1)}, u32[]{:S(2)}, u32[]{:S(2)}) %collective-permute-start.22) | collective-permute-done | bytes 1310752 | tf_op jit(solution)/shard_map/ppermute | solution.py:951
  268.5 3.1 collective-permute-start.25
  276.4 4.1 %collective-permute-done.24 = f32[32,512]{1,0:T(8,128)S(1)} collective-permute-done((f32[32,512]{1,0:T(8,128)S(1)}, f32[32,512]{1,0:T(8,128)S(1)}, u32[]{:S(2)}, u32[]{:S(2)}) %collective-permute-start.24) | collective-permute-done | bytes 65568 | tf_op jit(solution)/shard_map/ppermute | solution.py:951
  281.4 4.0 %collective-permute-start.28 = (bf16[1,1280,128]{2,1,0:T(8,128)(2,1)S(1)}, bf16[1,1280,128]{2,1,0:T(8,128)(2,1)S(1)}, u32[]{:S(2)}, u32[]{:S(2)}) collective-permute-start(bf16[1,1280,128]{2,1,0:T(8,128)(2,1)S(1)} %add_convert_fusion.7), channel_id=1, source_target_pairs={{1,17},{3,19},{5,21},{7,23},{9,25},{11,27},{13,29},{15,31},{17,1},... | collective-permute-start | bytes 983048 | tf_op jit(solution)/shard_map/ppermute | solution.py:951
  288.6 5.0 %collective-permute-done.28 = bf16[1,1280,128]{2,1,0:T(8,128)(2,1)S(1)} collective-permute-done((bf16[1,1280,128]{2,1,0:T(8,128)(2,1)S(1)}, bf16[1,1280,128]{2,1,0:T(8,128)(2,1)S(1)}, u32[]{:S(2)}, u32[]{:S(2)}) %collective-permute-start.28) | collective-permute-done | bytes 327712 | tf_op jit(solution)/shard_map/ppermute | solution.py:951
  297.3 5.0 %collective-permute-done.29 = f32[32,512]{1,0:T(8,128)S(1)} collective-permute-done((f32[32,512]{1,0:T(8,128)S(1)}, f32[32,512]{1,0:T(8,128)S(1)}, u32[]{:S(2)}, u32[]{:S(2)}) %collective-permute-start.29) | collective-permute-done | bytes 65568 | tf_op jit(solution)/shard_map/ppermute | solution.py:951
  (176 shorter events, 69.1 us)
Async XLA Ops:
  3.6 21.6 %collective-permute-start.1 = (bf16[512,1536]{1,0:T(8,128)(2,1)}, bf16[512,1536]{1,0:T(8,128)(2,1)}, u32[]{:S(2)}, u32[]{:S(2)}) collective-permute-start(bf16[512,1536]{1,0:T(8,128)(2,1)} %dynamic-slice_bitcast_fusion), channel_id=1, source_target_pairs={{1,3},{2,0},{5,7},{6,4},{9,11},{10,8},{13,15},{14,12},{17,19},{18,... | collective-permute-start | bytes 4718600 | tf_op jit(solution)/shard_map/ppermute | solution.py:951
  13.5 41.6 %collective-permute-start = (bf16[1024,1536]{1,0:T(8,128)(2,1)S(1)}, bf16[1024,1536]{1,0:T(8,128)(2,1)S(1)}, u32[]{:S(2)}, u32[]{:S(2)}) collective-permute-start(bf16[1024,1536]{1,0:T(8,128)(2,1)S(1)} %bitcast.95), channel_id=1, source_target_pairs={{0,1},{1,0},{2,3},{3,2},{4,5},{5,4},{6,7},{7,6},{8,9},{9,8},{10,11... | collective-permute-start | bytes 9437192 | tf_op jit(solution)/shard_map/ppermute | solution.py:951
  26.0 22.0 %collective-permute-start.3 = (bf16[816,512]{1,0:T(8,128)(2,1)}, bf16[816,512]{1,0:T(8,128)(2,1)S(1)}, u32[]{:S(2)}, u32[]{:S(2)}) collective-permute-start(bf16[816,512]{1,0:T(8,128)(2,1)} %get-tuple-element.76.refs_6_.refs_10_.refs_13_), channel_id=1, source_target_pairs={{0,2},{1,3},{2,0},{3,1},{4,6},{5,7},{6,4},{7,5},{8,10},{9,11},{10,... | collective-permute-start | bytes 2506760 | tf_op jit(solution)/shard_map/ppermute | solution.py:951
  30.3 24.8 %collective-permute-start.6 = (bf16[512,1536]{1,0:T(8,128)(2,1)}, bf16[512,1536]{1,0:T(8,128)(2,1)S(1)}, u32[]{:S(2)}, u32[]{:S(2)}) collective-permute-start(bf16[512,1536]{1,0:T(8,128)(2,1)} %collective-permute-done.1.refs_2_.refs_6_.refs_5_), channel_id=1, source_target_pairs={{0,1},{3,2},{4,5},{7,6},{8,9},{11,10},{12,13},{15,14},{16,17},{19,... | collective-permute-start | bytes 4718600 | tf_op jit(solution)/shard_map/ppermute | solution.py:951
  31.6 23.5 %collective-permute-start.7 = (bf16[512,1536]{1,0:T(8,128)(2,1)S(1)}, bf16[512,1536]{1,0:T(8,128)(2,1)S(1)}, u32[]{:S(2)}, u32[]{:S(2)}) collective-permute-start(bf16[512,1536]{1,0:T(8,128)(2,1)S(1)} %collective-permute-done.5.refs_3_.refs_7_.refs_6_), channel_id=1, source_target_pairs={{0,1},{3,2},{4,5},{7,6},{8,9},{11,10},{12,13},{15,14},{16,17},{19,... | collective-permute-start | bytes 4718600 | tf_op jit(solution)/shard_map/ppermute | solution.py:951
  48.0 7.1 %collective-permute-start.8 = (bf16[816,512]{1,0:T(8,128)(2,1)S(1)}, bf16[816,512]{1,0:T(8,128)(2,1)S(1)}, u32[]{:S(2)}, u32[]{:S(2)}) collective-permute-start(bf16[816,512]{1,0:T(8,128)(2,1)S(1)} %collective-permute-done.3.refs_8_.refs_12_.refs_15_), channel_id=1, source_target_pairs={{0,1},{1,0},{2,3},{3,2},{4,5},{5,4},{6,7},{7,6},{8,9},{9,8},{10,11... | collective-permute-start | bytes 2506760 | tf_op jit(solution)/shard_map/ppermute | solution.py:951
  51.2 38.1 %collective-permute-start.4 = (bf16[1024,1536]{1,0:T(8,128)(2,1)S(1)}, bf16[1024,1536]{1,0:T(8,128)(2,1)}, u32[]{:S(2)}, u32[]{:S(2)}) collective-permute-start(bf16[1024,1536]{1,0:T(8,128)(2,1)S(1)} %bitcast.96), channel_id=1, source_target_pairs={{0,2},{3,1},{4,6},{7,5},{8,10},{11,9},{12,14},{15,13},{16,18},{19,... | collective-permute-start | bytes 9437192 | tf_op jit(solution)/shard_map/ppermute | solution.py:951
  89.3 6.9 %collective-permute-start.9 = (bf16[1024,1536]{1,0:T(8,128)(2,1)}, bf16[1024,1536]{1,0:T(8,128)(2,1)}, u32[]{:S(2)}, u32[]{:S(2)}) collective-permute-start(bf16[1024,1536]{1,0:T(8,128)(2,1)} %collective-permute-done.4.refs_2_.refs_11_), channel_id=1, source_target_pairs={{1,0},{2,3},{5,4},{6,7},{9,8},{10,11},{13,12},{14,15},{17,16},{18,... | collective-permute-start | bytes 9437192 | tf_op jit(solution)/shard_map/ppermute | solution.py:951
  150.0 10.3 %collective-permute-start.10 = (bf16[2,8,1024,128]{3,2,1,0:T(8,128)(2,1)}, bf16[2,8,1024,128]{3,2,1,0:T(8,128)(2,1)}, u32[]{:S(2)}, u32[]{:S(2)}) collective-permute-start(bf16[2,8,1024,128]{3,2,1,0:T(8,128)(2,1)} %get-tuple-element.95), channel_id=1, source_target_pairs={{0,1},{1,0},{2,3},{3,2},{4,5},{5,4},{6,7},{7,6},{8,9},{9,8},{10,11... | collective-permute-start | bytes 12582920 | tf_op jit(solution)/shard_map/ppermute | solution.py:951
  165.2 35.9 %collective-permute-start.13 = (bf16[4,1024,128]{2,1,0:T(8,128)(2,1)}, bf16[4,1024,128]{2,1,0:T(8,128)(2,1)S(1)}, u32[]{:S(2)}, u32[]{:S(2)}) collective-permute-start(bf16[4,1024,128]{2,1,0:T(8,128)(2,1)} %get-tuple-element.171.refs_0_), channel_id=1, source_target_pairs={{0,2},{1,3},{2,0},{3,1},{4,6},{5,7},{6,4},{7,5},{8,10},{9,11},{10,... | collective-permute-start | bytes 3145736 | tf_op jit(solution)/shard_map/ppermute | solution.py:951
  166.5 34.5 %collective-permute-start.14 = (bf16[4,1024,128]{2,1,0:T(8,128)(2,1)}, bf16[4,1024,128]{2,1,0:T(8,128)(2,1)S(1)}, u32[]{:S(2)}, u32[]{:S(2)}) collective-permute-start(bf16[4,1024,128]{2,1,0:T(8,128)(2,1)} %get-tuple-element.170.refs_1_), channel_id=1, source_target_pairs={{0,5},{1,4},{2,7},{3,6},{4,1},{5,0},{6,3},{7,2},{8,13},{9,12},{10,... | collective-permute-start | bytes 3145736 | tf_op jit(solution)/shard_map/ppermute | solution.py:951
  168.8 46.9 %collective-permute-start.15 = (bf16[4,1024,128]{2,1,0:T(8,128)(2,1)S(1)}, bf16[4,1024,128]{2,1,0:T(8,128)(2,1)S(1)}, u32[]{:S(2)}, u32[]{:S(2)}) collective-permute-start(bf16[4,1024,128]{2,1,0:T(8,128)(2,1)S(1)} %get-tuple-element.169.refs_2_), channel_id=1, source_target_pairs={{0,7},{1,6},{2,5},{3,4},{4,3},{5,2},{6,1},{7,0},{8,15},{9,14},{10,... | collective-permute-start | bytes 3145736 | tf_op jit(solution)/shard_map/ppermute | solution.py:951
  215.7 15.3 %collective-permute-start.17 = (bf16[8,1280,128]{2,1,0:T(8,128)(2,1)}, bf16[8,1280,128]{2,1,0:T(8,128)(2,1)S(1)}, u32[]{:S(2)}, u32[]{:S(2)}) collective-permute-start(bf16[8,1280,128]{2,1,0:T(8,128)(2,1)} %get-tuple-element.115), channel_id=1, source_target_pairs={{0,1},{1,0},{2,3},{3,2},{4,5},{5,4},{6,7},{7,6},{8,9},{9,8},{10,11... | collective-permute-start | bytes 7864328 | tf_op jit(solution)/shard_map/ppermute | solution.py:951
  216.5 14.5 %collective-permute-start.18 = (bf16[2,1024,128]{2,1,0:T(8,128)(2,1)S(1)}, bf16[2,1024,128]{2,1,0:T(8,128)(2,1)S(1)}, u32[]{:S(2)}, u32[]{:S(2)}) collective-permute-start(bf16[2,1024,128]{2,1,0:T(8,128)(2,1)S(1)} %get-tuple-element.177), channel_id=1, source_target_pairs={{0,8},{1,9},{2,10},{3,11},{4,12},{5,13},{6,14},{7,15},{8,0},{9,1},... | collective-permute-start | bytes 1572872 | tf_op jit(solution)/shard_map/ppermute | solution.py:951
  231.8 18.8 %collective-permute-start.20 = (bf16[4,1280,128]{2,1,0:T(8,128)(2,1)S(1)}, bf16[4,1280,128]{2,1,0:T(8,128)(2,1)S(1)}, u32[]{:S(2)}, u32[]{:S(2)}) collective-permute-start(bf16[4,1280,128]{2,1,0:T(8,128)(2,1)S(1)} %get-tuple-element.175), channel_id=1, source_target_pairs={{1,3},{3,1},{5,7},{7,5},{9,11},{11,9},{13,15},{15,13},{17,19},{19,... | collective-permute-start | bytes 3932168 | tf_op jit(solution)/shard_map/ppermute | solution.py:951
  233.9 18.9 %collective-permute-start.21 = (bf16[4,1280,128]{2,1,0:T(8,128)(2,1)S(1)}, bf16[4,1280,128]{2,1,0:T(8,128)(2,1)S(1)}, u32[]{:S(2)}, u32[]{:S(2)}) collective-permute-start(bf16[4,1280,128]{2,1,0:T(8,128)(2,1)S(1)} %bitcast.100), channel_id=1, source_target_pairs={{0,5},{2,7},{4,1},{6,3},{8,13},{10,15},{12,9},{14,11},{16,21},{18,... | collective-permute-start | bytes 3932168 | tf_op jit(solution)/shard_map/ppermute | solution.py:951
  235.2 32.6 %collective-permute-start.22 = (bf16[4,1280,128]{2,1,0:T(8,128)(2,1)S(1)}, bf16[4,1280,128]{2,1,0:T(8,128)(2,1)S(1)}, u32[]{:S(2)}, u32[]{:S(2)}) collective-permute-start(bf16[4,1280,128]{2,1,0:T(8,128)(2,1)S(1)} %get-tuple-element.175), channel_id=1, source_target_pairs={{0,7},{2,5},{4,3},{6,1},{8,15},{10,13},{12,11},{14,9},{16,23},{18,... | collective-permute-start | bytes 3932168 | tf_op jit(solution)/shard_map/ppermute | solution.py:951
  236.8 13.7 %collective-permute-start.23 = (bf16[1,1024,128]{2,1,0:T(8,128)(2,1)S(1)}, bf16[1,1024,128]{2,1,0:T(8,128)(2,1)S(1)}, u32[]{:S(2)}, u32[]{:S(2)}) collective-permute-start(bf16[1,1024,128]{2,1,0:T(8,128)(2,1)S(1)} %add_convert_fusion.9), channel_id=1, source_target_pairs={{0,16},{1,17},{2,18},{3,19},{4,20},{5,21},{6,22},{7,23},{8,24},{9,... | collective-permute-start | bytes 786440 | tf_op jit(solution)/shard_map/ppermute | solution.py:951
  268.5 12.7 %collective-permute-start.25 = (bf16[2,1280,128]{2,1,0:T(8,128)(2,1)S(1)}, bf16[2,1280,128]{2,1,0:T(8,128)(2,1)S(1)}, u32[]{:S(2)}, u32[]{:S(2)}) collective-permute-start(bf16[2,1280,128]{2,1,0:T(8,128)(2,1)S(1)} %get-tuple-element.173), channel_id=1, source_target_pairs={{1,9},{3,11},{5,13},{7,15},{9,1},{11,3},{13,5},{15,7},{17,25},{19,... | collective-permute-start | bytes 1966088 | tf_op jit(solution)/shard_map/ppermute | solution.py:951
  271.8 8.8 %collective-permute-start.26 = (bf16[1024,128]{1,0:T(8,128)(2,1)S(1)}, bf16[1024,128]{1,0:T(8,128)(2,1)S(1)}, u32[]{:S(2)}, u32[]{:S(2)}) collective-permute-start(bf16[1024,128]{1,0:T(8,128)(2,1)S(1)} %get-tuple-element.166), channel_id=1, source_target_pairs={{0,2},{1,3},{4,6},{5,7},{8,10},{9,11},{12,14},{13,15},{16,18},{17,... | collective-permute-start | bytes 786440 | tf_op jit(solution)/shard_map/ppermute | solution.py:951
  274.1 6.5 %collective-permute-start.24 = (f32[32,512]{1,0:T(8,128)S(1)}, f32[32,512]{1,0:T(8,128)S(1)}, u32[]{:S(2)}, u32[]{:S(2)}) collective-permute-start(f32[32,512]{1,0:T(8,128)S(1)} %add.147), channel_id=1, source_target_pairs={{0,16},{1,17},{2,18},{3,19},{4,20},{5,21},{6,22},{7,23},{8,24},{9,... | collective-permute-start | bytes 196616 | tf_op jit(solution)/shard_map/ppermute | solution.py:951
  281.4 12.2 %collective-permute-start.28 = (bf16[1,1280,128]{2,1,0:T(8,128)(2,1)S(1)}, bf16[1,1280,128]{2,1,0:T(8,128)(2,1)S(1)}, u32[]{:S(2)}, u32[]{:S(2)}) collective-permute-start(bf16[1,1280,128]{2,1,0:T(8,128)(2,1)S(1)} %add_convert_fusion.7), channel_id=1, source_target_pairs={{1,17},{3,19},{5,21},{7,23},{9,25},{11,27},{13,29},{15,31},{17,1},... | collective-permute-start | bytes 983048 | tf_op jit(solution)/shard_map/ppermute | solution.py:951
  293.7 8.5 %collective-permute-start.30 = (bf16[1280,128]{1,0:T(8,128)(2,1)S(1)}, bf16[1280,128]{1,0:T(8,128)(2,1)S(1)}, u32[]{:S(2)}, u32[]{:S(2)}) collective-permute-start(bf16[1280,128]{1,0:T(8,128)(2,1)S(1)} %bitcast.105), channel_id=1, source_target_pairs={{3,1},{7,5},{11,9},{15,13},{19,17},{23,21},{27,25},{31,29}} | collective-permute-start | bytes 983048 | tf_op jit(solution)/shard_map/ppermute | solution.py:951
  295.0 7.2 %collective-permute-start.29 = (f32[32,512]{1,0:T(8,128)S(1)}, f32[32,512]{1,0:T(8,128)S(1)}, u32[]{:S(2)}, u32[]{:S(2)}) collective-permute-start(f32[32,512]{1,0:T(8,128)S(1)} %add.159), channel_id=1, source_target_pairs={{0,2},{1,3},{2,0},{3,1},{4,6},{5,7},{6,4},{7,5},{8,10},{9,11},{10,... | collective-permute-start | bytes 196616 | tf_op jit(solution)/shard_map/ppermute | solution.py:951
  (43 other events, 499.3 us)

commit v2 on v1

--- a/solution.py
+++ b/solution.py
@@ -313,7 +313,7 @@
 
 def fill_taps(z, taps, mask, layer):
     dilation = 2**layer
-    rows = 32
+    rows = 128
 
     def one(i, _):
         begin = pl.multiple_of(i * rows, rows)
@@ -551,29 +551,27 @@
         )
         x_in = [copies.start(x_ref, all_taps.at[0, pl.ds(z.taps, z.x_rows)])]
         if not last:
-            gate_in += [copies.start(h_in, hs.at[0])]
+            gate_in += [copies.start(h_in, hs.at[0, :, pl.ds(0, z.res)])]
             gate_in += [copies.start(a, b.at[0]) for a, b in zip(saved_high[1:], (fa_vs, fb_vs))]
             mix_in = [copies.start(saved_high[0], gated_vs.at[0]), copies.start(dx_in, dx_ref)]
-        else:
-            mix_in = [copies.start(a, spare.at[i]) for i, a in enumerate(other_gated[:2])]
-        turned_copy = copies.start(turned_in, turned)
-        low_k = 0 if first else 1
-        if first:
-            in_copies = taps_copies(z, s_ref, sources[0], 0, in_v, sems.at[copies.used])
-            copies.used += 1
-            low_x = all_taps.at[0, pl.ds(z.taps, z.x_rows)]
-            pack_low, taps_low = copies.weights(z, s_ref, None, packs, 0, low_wide, mes.at[1], 0)
-            each(in_copies, "start")
-            low_in = []
-        else:
-            low_x = all_taps.at[1, pl.ds(z.taps, z.x_rows)]
-            low_in = [copies.start(stream_low, all_taps.at[1, pl.ds(z.res, z.res)])]
-            pack_low, taps_low = copies.weights(
-                z, s_ref, sources[low], packs, low, wides.at[1], mes.at[1], z.taps
-            )
-            x_in.append(copies.start(x_ref, low_x))
-        gate_low = [copies.start(a, b.at[1]) for a, b in zip(saved_low[1:], (fa_vs, fb_vs))]
-        mix_low = copies.start(saved_low[0], gated_vs.at[1])
+        low_x = all_taps.at[0 if first else 1, pl.ds(z.taps, z.x_rows)]
+
+        def fetch_low():
+            turned_copy = copies.start(turned_in, turned)
+            gate = [copies.start(a, b.at[1]) for a, b in zip(saved_low[1:], (fa_vs, fb_vs))]
+            gate.append(copies.start(saved_low[0], gated_vs.at[1]))
+            if first:
+                pack, taps = copies.weights(z, s_ref, None, packs, 0, low_wide, mes.at[1], 0)
+                taps = taps_copies(z, s_ref, sources[0], 0, in_v, sems.at[copies.used])
+                copies.used += 1
+                each(taps, "start")
+                return turned_copy, gate, [], pack, taps
+            fill = [
+                copies.start(stream_low, all_taps.at[1, pl.ds(z.res, z.res)]),
+                copies.start(x_ref, low_x),
+            ]
+            pack, taps = copies.weights(z, s_ref, sources[low], packs, low, wides.at[1], mes.at[1], z.taps)
+            return turned_copy, gate, fill, pack, taps
 
         for k in range(2):
             mes[k, z.pack_cond :, :] = jnp.zeros((z.me_rows - z.pack_cond, z.res), BF)
@@ -586,6 +584,8 @@
         each(pack_high, "wait")
         if last:
             each(taps_high, "wait")
+            mix_in = [copies.start(a, spare.at[i]) for i, a in enumerate(other_gated[:2])]
+            turned_copy, gate_low, low_in, pack_low, taps_low = fetch_low()
             lu = lu_ref[...]
             r = lax.broadcasted_iota(jnp.int32, lu.shape, 0)
             c = lax.broadcasted_iota(jnp.int32, lu.shape, 1)
@@ -612,7 +612,10 @@
         else:
             for copy in gate_in:
                 copy.wait()
+            turned_copy, gate_low, low_in, pack_low, taps_low = fetch_low()
             leaving = []
+        for k in range(2):
+            hs[k, :, z.res :] = dres_ref[...]
 
         two = lambda exact: jnp.concatenate(
             [exact.astype(BF).astype(F32), exact - exact.astype(BF).astype(F32)], axis=0
@@ -621,26 +624,25 @@
         end_bias = mm(two(jnp.concatenate([dsum, jnp.zeros((7, LANES), F32)], axis=0)), end_ref[16:, :])
         end_bias = end_bias[0:8] + end_bias[8:16]
 
-        def gate_and_mix(layer, k, h_ref, grad_rows, at, ready):
+        def gate_and_mix(k, hd, has_h, grad_rows, at, ready):
+            begin = 0 if has_h else z.res
             me = mes.at[k]
             for n in range(z.res // width):
                 cols = slice(n * width, (n + 1) * width)
-                dgated = mm(dres_ref[...], me[z.res :, cols])
-                if h_ref is not None:
-                    dgated = dgated + mm(h_ref[...], me[0 : z.res, cols])
+                dgated = mm(hd[:, begin:], me[begin:, cols])
                 dpre[:, cols] = (dgated * fa_vs[k, :, cols].astype(F32)).astype(BF)
                 dpre[:, z.res + n * width : z.res + (n + 1) * width] = (
                     dgated * fb_vs[k, :, cols].astype(F32)
                 ).astype(BF)
             for copy in ready:
                 copy.wait()
-            outer = mm(gated_vs[k], dres_ref[...]).T[0 : z.group]
+            both = mm(gated_vs[k], hd[:, begin:])
+            outer = both[:, z.res - begin :].T[0 : z.group]
             mix_grad = mm(end_ref[0:16, :], two(outer), 0, 0)
             bias_grad = end_bias
-            if h_ref is not None:
-                h_mix = mm(gated_vs[k], h_ref[...]).T
-                mix_grad = mix_grad + jnp.concatenate([h_mix, jnp.zeros((z.skip, z.res), F32)], axis=0)
-                h_sum = jnp.sum(h_ref[...].astype(F32), axis=0, keepdims=True)
+            if has_h:
+                mix_grad = mix_grad + jnp.concatenate([both[:, 0 : z.res].T, jnp.zeros((z.skip, z.res), F32)], axis=0)
+                h_sum = jnp.sum(hd[:, 0 : z.res].astype(F32), axis=0, keepdims=True)
                 h_sum = jnp.concatenate([h_sum, jnp.zeros((7, z.res), F32)], axis=0)
                 bias_grad = bias_grad + jnp.concatenate([h_sum, jnp.zeros((8, z.skip), F32)], axis=1)
             mix_grad = mix_grad.astype(BF)
@@ -725,7 +727,7 @@
                 new_h[:, cols] = result.astype(BF)
 
         h_high = None if last else hs.at[0]
-        outer, bias_grad = gate_and_mix(high, 0, h_high, grads, z.taps + z.x_rows, [] if last else mix_in)
+        outer, bias_grad = gate_and_mix(0, hs.at[0], not last, grads, z.taps + z.x_rows, [] if last else mix_in)
         if last:
             p_ref[high, :, :] = outer
             a_ref[...] = mm(all_taps[0, z.taps :, :], dres_ref[...]).T[0 : z.group]
@@ -749,24 +751,24 @@
             copy.wait()
         sent_wait(grads, half_rows)
         if not first:
-            outer, bias_grad = gate_and_mix(low, 1, hs.at[1], grads, z.taps + z.x_rows, [mix_low])
+            outer, bias_grad = gate_and_mix(1, hs.at[1], True, grads, z.taps + z.x_rows, [])
             if last:
                 p_ref[low, :, :] = outer
             taps_gradients(1, bias_grad)
             send(low, grads, half_rows, 0)
             each(taps_low, "wait")
             stream_gradient(low, 1, hs.at[1], hs.at[0])
-            leaving += [copies.start(hs.at[0], h_out), copies.start(dx_ref, dx_out)]
+            leaving += [copies.start(hs.at[0, :, pl.ds(0, z.res)], h_out), copies.start(dx_ref, dx_out)]
             sent_wait(grads, half_rows)
         else:
-            outer, bias_grad = gate_and_mix(0, 1, hs.at[1], low_grads, z.x_rows, [mix_low])
+            outer, bias_grad = gate_and_mix(1, hs.at[1], True, low_grads, z.x_rows, [])
             dcond = mm(low_x[...], dpre[...])
             for s in range(z.blocks):
                 low_grads[s, 0 : z.x_rows, :] = with_bias(dcond[:, s * LANES : (s + 1) * LANES], bias_grad, s)
             send(0, low_grads, extra, half_rows)
             h = z.half
-            g_first = hs.at[0]
-            g_first[...] = (hs[1].astype(F32) + mm(dres_ref[...], end_ref[16:, 0 : z.res])).astype(BF)
+            g_first = hs.at[0, :, pl.ds(0, z.res)]
+            g_first[...] = (hs[1, :, 0 : z.res].astype(F32) + mm(dres_ref[...], end_ref[16:, 0 : z.res])).astype(BF)
             dx = dx_ref[...] + mm(dpre[...], low_wide[...]) + mm(g_first[...], sx_ref[0 : z.res, :])
             dx = dx.T
             hx = mm(low_x[...], g_first[...])
@@ -779,7 +781,7 @@
                 folded(dcond, 0) + folded(dcond, 1) + folded(dcond, 2) + [jnp.zeros((16 - 3 * (h + 1), z.gate), F32)],
                 axis=0,
             )
-            each(in_copies, "wait")
+            each(taps_low, "wait")
             back = mm(two(q), in_v[...])
             start_rows = jnp.concatenate(folded(hx, 1), axis=0)
             for tap in range(3):
@@ -877,7 +879,7 @@
         pltpu.VMEM((2, z.frames, z.res), BF),
         pltpu.VMEM((z.frames, z.gate), BF),
         pltpu.VMEM((z.blocks, z.share_rows, LANES), BF),
-        pltpu.VMEM((2, z.frames, z.res), BF),
+        pltpu.VMEM((2, z.frames, z.me_rows), BF),
         pltpu.VMEM((z.frames, z.x_rows), F32),
         pltpu.VMEM((z.frames, z.x_rows), F32),
         pltpu.VMEM((z.frames, LANES), BF),
@@ -1218,6 +1220,8 @@
     if z.direct:
         both = Chain(reduce_first_two(z, *blocks[1]))
         active += [both, pair]
+        for group in ((both, small), (pair, small), (pair, small)):
+            token = advance(group, *token)
     while any(chain.arriving for chain in active):
         token = advance(active, *token)
     whole_sum = small.result

time: 317 us -> 301 us (0.950)
  the two profiles are of different devices: /device:TPU:1 before, /device:TPU:0 now
where the time goes in v2:
time: 301 us; the launch traced here: 295 us
  Pallas kernels  113 us (38%)
  waiting for transfers between devices  106 us (35%)
  starting transfers between devices  45 us (15%)
  local copies, waits for them, and re-layouts  15.6 us (5%)
  other arithmetic  12.4 us (4%)
    ppermute x32, waiting for transfers between devices, permute(): return lax.ppermute(block, ('dp', 'layer'), pairs)  106 us
    pallas_call x2, Pallas kernels, per_device(): stay, cross, *outs = kernel(scalars, *ins)  80.6 us
    ppermute x32, starting transfers between devices, permute(): return lax.ppermute(block, ('dp', 'layer'), pairs)  45 us
    pallas_call x1, Pallas kernels, per_device(): forward_group(z, len(early), len(packs))  23.9 us
    unnamed x70, local copies, waits for them, and re-layouts  6.94 us
  transfers between devices with their start and end apart: 32, of which 13 were waited for; matrix products, arithmetic and copies ran while one was open for 3% of the time, Pallas kernels for 22%

profile of v2, /device:TPU:0, one launch (start us, length us, event | category | flops | bytes accessed | tf_op | source)
XLA Modules:
  0.0 295.3 jit_solution(839583546192051748)
XLA Ops:
  0.7 2.9 dynamic-slice_bitcast_fusion
  7.4 5.4 %prepare_weights.1 = (bf16[816,512]{1,0:T(8,128)(2,1)}, bf16[528,128]{1,0:T(8,128)(2,1)S(1)}) custom-call(s32[3]{0:T(128)S(1)} %pad_add_fusion.s_ref, bf16[1024,1536]{1,0:T(8,128)(2,1)S(1)} %bitcast.94, bf16[1024,80]{1,0:T(8,128)(2,1)S(1)} %bitcast.99, f32[1,1024]{1,0:T(1,128)S(1)} %copy-done.12, bf16[768,512]{1,0:T(8,128)(2,1)S(1)} %bitcast.97, ...), custom_call_target="tpu_custom_call" | custom-call | flops 402653184 | bytes 6291456 | tf_op jit(solution)/shard_map/prepare_weights/pallas_call | solution.py:1155
  14.1 2.6 prepare_frames.1
  17.3 9.2 %collective-permute-done.1.refs_2_.refs_6_.refs_5_ = bf16[512,1536]{1,0:T(8,128)(2,1)} collective-permute-done((bf16[512,1536]{1,0:T(8,128)(2,1)}, bf16[512,1536]{1,0:T(8,128)(2,1)}, u32[]{:S(2)}, u32[]{:S(2)}) %collective-permute-start.1) | collective-permute-done | bytes 1572896 | tf_op jit(solution)/shard_map/ppermute | solution.py:953
  26.5 4.5 %collective-permute-start.5 = (bf16[512,1536]{1,0:T(8,128)(2,1)}, bf16[512,1536]{1,0:T(8,128)(2,1)S(1)}, u32[]{:S(2)}, u32[]{:S(2)}) collective-permute-start(bf16[512,1536]{1,0:T(8,128)(2,1)} %collective-permute-done.1.refs_2_.refs_6_.refs_5_), channel_id=1, source_target_pairs={{0,4},{3,7},{4,0},{7,3},{8,12},{11,15},{12,8},{15,11},{16,20},{19,... | collective-permute-start | bytes 4718600 | tf_op jit(solution)/shard_map/ppermute | solution.py:953
  32.8 16.9 %collective-permute-done.5.refs_3_.refs_7_.refs_6_ = bf16[512,1536]{1,0:T(8,128)(2,1)S(1)} collective-permute-done((bf16[512,1536]{1,0:T(8,128)(2,1)}, bf16[512,1536]{1,0:T(8,128)(2,1)S(1)}, u32[]{:S(2)}, u32[]{:S(2)}) %collective-permute-start.5) | collective-permute-done | bytes 1572896 | tf_op jit(solution)/shard_map/ppermute | solution.py:953
  51.1 4.3 %collective-permute-start.4 = (bf16[1024,1536]{1,0:T(8,128)(2,1)S(1)}, bf16[1024,1536]{1,0:T(8,128)(2,1)}, u32[]{:S(2)}, u32[]{:S(2)}) collective-permute-start(bf16[1024,1536]{1,0:T(8,128)(2,1)S(1)} %bitcast.96), channel_id=1, source_target_pairs={{0,2},{3,1},{4,6},{7,5},{8,10},{11,9},{12,14},{15,13},{16,18},{19,... | collective-permute-start | bytes 9437192 | tf_op jit(solution)/shard_map/ppermute | solution.py:953
  58.3 23.9 %forward_group.1 = (bf16[512,1536]{1,0:T(8,128)(2,1)}, bf16[1536,512]{1,0:T(8,128)(2,1)}, bf16[1536,512]{1,0:T(8,128)(2,1)}, bf16[512,1536]{1,0:T(8,128)(2,1)}, ...) custom-call(s32[3]{0:T(128)S(1)} %pad_add_fusion.s_ref, ...), custom_call_target="tpu_custom_call" | custom-call | flops 57982058496 | bytes 41943040 | tf_op jit(solution)/shard_map/forward_group/pallas_call | solution.py:1166
  82.2 6.2 %collective-permute-done.4.refs_2_.refs_11_ = bf16[1024,1536]{1,0:T(8,128)(2,1)} collective-permute-done((bf16[1024,1536]{1,0:T(8,128)(2,1)S(1)}, bf16[1024,1536]{1,0:T(8,128)(2,1)}, u32[]{:S(2)}, u32[]{:S(2)}) %collective-permute-start.4) | collective-permute-done | bytes 3145760 | tf_op jit(solution)/shard_map/ppermute | solution.py:953
  91.3 5.2 %collective-permute-done.9.refs_3_.refs_12_ = bf16[1024,1536]{1,0:T(8,128)(2,1)} collective-permute-done((bf16[1024,1536]{1,0:T(8,128)(2,1)}, bf16[1024,1536]{1,0:T(8,128)(2,1)}, u32[]{:S(2)}, u32[]{:S(2)}) %collective-permute-start.9) | collective-permute-done | bytes 3145760 | tf_op jit(solution)/shard_map/ppermute | solution.py:953
  96.5 48.5 %gradient_last.1 = (bf16[2,8,1024,128]{3,2,1,0:T(8,128)(2,1)}, bf16[2,8,1024,128]{3,2,1,0:T(8,128)(2,1)}, bf16[1536,512]{1,0:T(8,128)(2,1)}, f32[1536,128]{1,0:T...) custom-call(s32[3]{0:T(128)} %copy-done.10, ...), custom_call_target="tpu_custom_call" | custom-call | flops 144955146240 | bytes 20971520 | tf_op jit(solution)/shard_map/gradient_last/pallas_call | solution.py:1196
  147.5 4.8 %collective-permute-done.11 = f32[2,16,512]{2,1,0:T(8,128)S(1)} collective-permute-done((f32[2,16,512]{2,1,0:T(8,128)S(1)}, f32[2,16,512]{2,1,0:T(8,128)S(1)}, u32[]{:S(2)}, u32[]{:S(2)}) %collective-permute-start.11) | collective-permute-done | bytes 65568 | tf_op jit(solution)/shard_map/ppermute | solution.py:953
  153.9 2.5 collective-permute-done.12
  156.4 5.1 %add_convert_fusion.2 = (bf16[1,4,1024,128]{3,2,1,0:T(8,128)(2,1)S(1)}, bf16[4,1024,128]{2,1,0:T(8,128)(2,1)}, bf16[4,1024,128]{2,1,0:T(8,128)(2,1)}, bf16[4,1024,128]{2,1,0:T(8,128)(2,1)}) fusion(bf16[2,8,1024,128]{3,2,1,0:T(8,128)(2,1)} %collective-permute-done.10, bf16[2,8,1024,128]{3,2,1,0:T(8,128)(2,1)} %get-tuple-element.94), kind=kLoop, calls=%fused_computation.2 | loop fusion | flops 8388608 | bytes 12582912 | tf_op jit(solution)/shard_map/convert_element_type | solution.py:1018
  164.7 32.1 %gradient_first.1 = (bf16[8,1280,128]{2,1,0:T(8,128)(2,1)}, bf16[8,1280,128]{2,1,0:T(8,128)(2,1)}, f32[16,512]{1,0:T(8,128)}, f32[80,1536]{1,0:T(8,128)}, f32[8,1536]{1,0:T(8,128)}) custom-call(s32[3]{0:T(128)} %copy-done.10, bf16[4,1024,128]{2,1,0:T(8,128)(2,1)} %get-tuple-element.171.refs_0_, bf16[4,1024,128]{2,1,0:T(8,128)(2,1)} %get-tuple-element.170.refs_1_, ...), custom_call_target="tpu_custom_call" | custom-call | flops 96636764160 | bytes 20971520 | tf_op jit(solution)/shard_map/gradient_first/pallas_call | solution.py:1196
  196.8 13.8 %collective-permute-done.15 = bf16[4,1024,128]{2,1,0:T(8,128)(2,1)S(1)} collective-permute-done((bf16[4,1024,128]{2,1,0:T(8,128)(2,1)}, bf16[4,1024,128]{2,1,0:T(8,128)(2,1)S(1)}, u32[]{:S(2)}, u32[]{:S(2)}) %collective-permute-start.15) | collective-permute-done | bytes 1048608 | tf_op jit(solution)/shard_map/ppermute | solution.py:953
  213.3 2.6 collective-permute-start.18
  217.4 5.2 %collective-permute-start.25 = (bf16[4,1280,128]{2,1,0:T(8,128)(2,1)S(1)}, bf16[4,1280,128]{2,1,0:T(8,128)(2,1)S(1)}, u32[]{:S(2)}, u32[]{:S(2)}) collective-permute-start(bf16[4,1280,128]{2,1,0:T(8,128)(2,1)S(1)} %get-tuple-element.175), channel_id=1, source_target_pairs={{0,7},{2,5},{4,3},{6,1},{8,15},{10,13},{12,11},{14,9},{16,23},{18,... | collective-permute-start | bytes 3932168 | tf_op jit(solution)/shard_map/ppermute | solution.py:953
  225.9 2.7 collective-permute-done.18
  229.6 2.8 collective-permute-start.20
  232.7 14.1 %collective-permute-done.21 = f32[32,512]{1,0:T(8,128)S(1)} collective-permute-done((f32[32,512]{1,0:T(8,128)S(1)}, f32[32,512]{1,0:T(8,128)S(1)}, u32[]{:S(2)}, u32[]{:S(2)}) %collective-permute-start.21) | collective-permute-done | bytes 65568 | tf_op jit(solution)/shard_map/ppermute | solution.py:953
  246.9 2.3 collective-permute-start.26
  250.3 4.1 %collective-permute-done.22 = f32[32,512]{1,0:T(8,128)S(1)} collective-permute-done((f32[32,512]{1,0:T(8,128)S(1)}, f32[32,512]{1,0:T(8,128)S(1)}, u32[]{:S(2)}, u32[]{:S(2)}) %collective-permute-start.22) | collective-permute-done | bytes 65568 | tf_op jit(solution)/shard_map/ppermute | solution.py:953
  266.3 24.2 %collective-permute-done.31 = bf16[512,128]{1,0:T(8,128)(2,1)S(1)} collective-permute-done((bf16[512,128]{1,0:T(8,128)(2,1)S(1)}, bf16[512,128]{1,0:T(8,128)(2,1)S(1)}, u32[]{:S(2)}, u32[]{:S(2)}) %collective-permute-start.31) | collective-permute-done | bytes 131104 | tf_op jit(solution)/shard_map/ppermute | solution.py:953
  (174 shorter events, 47.7 us)
Async XLA Ops:
  3.6 22.9 %collective-permute-start.1 = (bf16[512,1536]{1,0:T(8,128)(2,1)}, bf16[512,1536]{1,0:T(8,128)(2,1)}, u32[]{:S(2)}, u32[]{:S(2)}) collective-permute-start(bf16[512,1536]{1,0:T(8,128)(2,1)} %dynamic-slice_bitcast_fusion), channel_id=1, source_target_pairs={{1,3},{2,0},{5,7},{6,4},{9,11},{10,8},{13,15},{14,12},{17,19},{18,... | collective-permute-start | bytes 4718600 | tf_op jit(solution)/shard_map/ppermute | solution.py:953
  14.0 41.5 %collective-permute-start = (bf16[1024,1536]{1,0:T(8,128)(2,1)S(1)}, bf16[1024,1536]{1,0:T(8,128)(2,1)S(1)}, u32[]{:S(2)}, u32[]{:S(2)}) collective-permute-start(bf16[1024,1536]{1,0:T(8,128)(2,1)S(1)} %bitcast.95), channel_id=1, source_target_pairs={{0,1},{1,0},{2,3},{3,2},{4,5},{5,4},{6,7},{7,6},{8,9},{9,8},{10,11... | collective-permute-start | bytes 9437192 | tf_op jit(solution)/shard_map/ppermute | solution.py:953
  26.5 23.1 %collective-permute-start.5 = (bf16[512,1536]{1,0:T(8,128)(2,1)}, bf16[512,1536]{1,0:T(8,128)(2,1)S(1)}, u32[]{:S(2)}, u32[]{:S(2)}) collective-permute-start(bf16[512,1536]{1,0:T(8,128)(2,1)} %collective-permute-done.1.refs_2_.refs_6_.refs_5_), channel_id=1, source_target_pairs={{0,4},{3,7},{4,0},{7,3},{8,12},{11,15},{12,8},{15,11},{16,20},{19,... | collective-permute-start | bytes 4718600 | tf_op jit(solution)/shard_map/ppermute | solution.py:953
  31.0 20.0 %collective-permute-start.3 = (bf16[816,512]{1,0:T(8,128)(2,1)}, bf16[816,512]{1,0:T(8,128)(2,1)S(1)}, u32[]{:S(2)}, u32[]{:S(2)}) collective-permute-start(bf16[816,512]{1,0:T(8,128)(2,1)} %get-tuple-element.76.refs_6_.refs_10_.refs_13_), channel_id=1, source_target_pairs={{0,2},{1,3},{2,0},{3,1},{4,6},{5,7},{6,4},{7,5},{8,10},{9,11},{10,... | collective-permute-start | bytes 2506760 | tf_op jit(solution)/shard_map/ppermute | solution.py:953
  31.1 24.3 %collective-permute-start.6 = (bf16[512,1536]{1,0:T(8,128)(2,1)}, bf16[512,1536]{1,0:T(8,128)(2,1)S(1)}, u32[]{:S(2)}, u32[]{:S(2)}) collective-permute-start(bf16[512,1536]{1,0:T(8,128)(2,1)} %collective-permute-done.1.refs_2_.refs_6_.refs_5_), channel_id=1, source_target_pairs={{0,1},{3,2},{4,5},{7,6},{8,9},{11,10},{12,13},{15,14},{16,17},{19,... | collective-permute-start | bytes 4718600 | tf_op jit(solution)/shard_map/ppermute | solution.py:953
  49.6 5.8 %collective-permute-start.7 = (bf16[512,1536]{1,0:T(8,128)(2,1)S(1)}, bf16[512,1536]{1,0:T(8,128)(2,1)S(1)}, u32[]{:S(2)}, u32[]{:S(2)}) collective-permute-start(bf16[512,1536]{1,0:T(8,128)(2,1)S(1)} %collective-permute-done.5.refs_3_.refs_7_.refs_6_), channel_id=1, source_target_pairs={{0,1},{3,2},{4,5},{7,6},{8,9},{11,10},{12,13},{15,14},{16,17},{19,... | collective-permute-start | bytes 4718600 | tf_op jit(solution)/shard_map/ppermute | solution.py:953
  51.1 37.3 %collective-permute-start.4 = (bf16[1024,1536]{1,0:T(8,128)(2,1)S(1)}, bf16[1024,1536]{1,0:T(8,128)(2,1)}, u32[]{:S(2)}, u32[]{:S(2)}) collective-permute-start(bf16[1024,1536]{1,0:T(8,128)(2,1)S(1)} %bitcast.96), channel_id=1, source_target_pairs={{0,2},{3,1},{4,6},{7,5},{8,10},{11,9},{12,14},{15,13},{16,18},{19,... | collective-permute-start | bytes 9437192 | tf_op jit(solution)/shard_map/ppermute | solution.py:953
  88.4 8.1 %collective-permute-start.9 = (bf16[1024,1536]{1,0:T(8,128)(2,1)}, bf16[1024,1536]{1,0:T(8,128)(2,1)}, u32[]{:S(2)}, u32[]{:S(2)}) collective-permute-start(bf16[1024,1536]{1,0:T(8,128)(2,1)} %collective-permute-done.4.refs_2_.refs_11_), channel_id=1, source_target_pairs={{1,0},{2,3},{5,4},{6,7},{9,8},{10,11},{13,12},{14,15},{17,16},{18,... | collective-permute-start | bytes 9437192 | tf_op jit(solution)/shard_map/ppermute | solution.py:953
  145.0 11.3 %collective-permute-start.10 = (bf16[2,8,1024,128]{3,2,1,0:T(8,128)(2,1)}, bf16[2,8,1024,128]{3,2,1,0:T(8,128)(2,1)}, u32[]{:S(2)}, u32[]{:S(2)}) collective-permute-start(bf16[2,8,1024,128]{3,2,1,0:T(8,128)(2,1)} %get-tuple-element.95), channel_id=1, source_target_pairs={{0,1},{1,0},{2,3},{3,2},{4,5},{5,4},{6,7},{7,6},{8,9},{9,8},{10,11... | collective-permute-start | bytes 12582920 | tf_op jit(solution)/shard_map/ppermute | solution.py:953
  147.1 5.2 %collective-permute-start.11 = (f32[2,16,512]{2,1,0:T(8,128)S(1)}, f32[2,16,512]{2,1,0:T(8,128)S(1)}, u32[]{:S(2)}, u32[]{:S(2)}) collective-permute-start(f32[2,16,512]{2,1,0:T(8,128)S(1)} %dynamic-slice_bitcast_fusion.1), channel_id=1, source_target_pairs={{0,1},{1,0},{2,3},{3,2},{4,5},{5,4},{6,7},{7,6},{8,9},{9,8},{10,11... | collective-permute-start | bytes 196616 | tf_op jit(solution)/shard_map/ppermute | solution.py:953
  161.5 35.3 %collective-permute-start.13 = (bf16[4,1024,128]{2,1,0:T(8,128)(2,1)}, bf16[4,1024,128]{2,1,0:T(8,128)(2,1)S(1)}, u32[]{:S(2)}, u32[]{:S(2)}) collective-permute-start(bf16[4,1024,128]{2,1,0:T(8,128)(2,1)} %get-tuple-element.171.refs_0_), channel_id=1, source_target_pairs={{0,2},{1,3},{2,0},{3,1},{4,6},{5,7},{6,4},{7,5},{8,10},{9,11},{10,... | collective-permute-start | bytes 3145736 | tf_op jit(solution)/shard_map/ppermute | solution.py:953
  162.9 33.9 %collective-permute-start.14 = (bf16[4,1024,128]{2,1,0:T(8,128)(2,1)}, bf16[4,1024,128]{2,1,0:T(8,128)(2,1)S(1)}, u32[]{:S(2)}, u32[]{:S(2)}) collective-permute-start(bf16[4,1024,128]{2,1,0:T(8,128)(2,1)} %get-tuple-element.170.refs_1_), channel_id=1, source_target_pairs={{0,5},{1,4},{2,7},{3,6},{4,1},{5,0},{6,3},{7,2},{8,13},{9,12},{10,... | collective-permute-start | bytes 3145736 | tf_op jit(solution)/shard_map/ppermute | solution.py:953
  162.9 47.7 %collective-permute-start.15 = (bf16[4,1024,128]{2,1,0:T(8,128)(2,1)}, bf16[4,1024,128]{2,1,0:T(8,128)(2,1)S(1)}, u32[]{:S(2)}, u32[]{:S(2)}) collective-permute-start(bf16[4,1024,128]{2,1,0:T(8,128)(2,1)} %get-tuple-element.169.refs_2_), channel_id=1, source_target_pairs={{0,7},{1,6},{2,5},{3,4},{4,3},{5,2},{6,1},{7,0},{8,15},{9,14},{10,... | collective-permute-start | bytes 3145736 | tf_op jit(solution)/shard_map/ppermute | solution.py:953
  210.6 5.4 %collective-permute-start.16 = (bf16[8,1280,128]{2,1,0:T(8,128)(2,1)}, bf16[8,1280,128]{2,1,0:T(8,128)(2,1)S(1)}, u32[]{:S(2)}, u32[]{:S(2)}) collective-permute-start(bf16[8,1280,128]{2,1,0:T(8,128)(2,1)} %get-tuple-element.115), channel_id=1, source_target_pairs={{0,1},{1,0},{2,3},{3,2},{4,5},{5,4},{6,7},{7,6},{8,9},{9,8},{10,11... | collective-permute-start | bytes 7864328 | tf_op jit(solution)/shard_map/ppermute | solution.py:953
  213.3 15.3 %collective-permute-start.18 = (bf16[2,1024,128]{2,1,0:T(8,128)(2,1)S(1)}, bf16[2,1024,128]{2,1,0:T(8,128)(2,1)S(1)}, u32[]{:S(2)}, u32[]{:S(2)}) collective-permute-start(bf16[2,1024,128]{2,1,0:T(8,128)(2,1)S(1)} %get-tuple-element.177), channel_id=1, source_target_pairs={{0,8},{1,9},{2,10},{3,11},{4,12},{5,13},{6,14},{7,15},{8,0},{9,1},... | collective-permute-start | bytes 1572872 | tf_op jit(solution)/shard_map/ppermute | solution.py:953
  216.6 37.8 %collective-permute-start.23 = (bf16[4,1280,128]{2,1,0:T(8,128)(2,1)S(1)}, bf16[4,1280,128]{2,1,0:T(8,128)(2,1)S(1)}, u32[]{:S(2)}, u32[]{:S(2)}) collective-permute-start(bf16[4,1280,128]{2,1,0:T(8,128)(2,1)S(1)} %get-tuple-element.175), channel_id=1, source_target_pairs={{1,3},{3,1},{5,7},{7,5},{9,11},{11,9},{13,15},{15,13},{17,19},{19,... | collective-permute-start | bytes 3932168 | tf_op jit(solution)/shard_map/ppermute | solution.py:953
  217.4 37.0 %collective-permute-start.25 = (bf16[4,1280,128]{2,1,0:T(8,128)(2,1)S(1)}, bf16[4,1280,128]{2,1,0:T(8,128)(2,1)S(1)}, u32[]{:S(2)}, u32[]{:S(2)}) collective-permute-start(bf16[4,1280,128]{2,1,0:T(8,128)(2,1)S(1)} %get-tuple-element.175), channel_id=1, source_target_pairs={{0,7},{2,5},{4,3},{6,1},{8,15},{10,13},{12,11},{14,9},{16,23},{18,... | collective-permute-start | bytes 3932168 | tf_op jit(solution)/shard_map/ppermute | solution.py:953
  222.6 31.8 %collective-permute-start.24 = (bf16[4,1280,128]{2,1,0:T(8,128)(2,1)S(1)}, bf16[4,1280,128]{2,1,0:T(8,128)(2,1)S(1)}, u32[]{:S(2)}, u32[]{:S(2)}) collective-permute-start(bf16[4,1280,128]{2,1,0:T(8,128)(2,1)S(1)} %bitcast.100), channel_id=1, source_target_pairs={{0,5},{2,7},{4,1},{6,3},{8,13},{10,15},{12,9},{14,11},{16,21},{18,... | collective-permute-start | bytes 3932168 | tf_op jit(solution)/shard_map/ppermute | solution.py:953
  224.0 5.5 %collective-permute-start.19 = (f32[32,512]{1,0:T(8,128)S(1)}, f32[32,512]{1,0:T(8,128)S(1)}, u32[]{:S(2)}, u32[]{:S(2)}) collective-permute-start(f32[32,512]{1,0:T(8,128)S(1)} %fusion.25), channel_id=1, source_target_pairs={{0,8},{1,9},{2,10},{3,11},{4,12},{5,13},{6,14},{7,15},{8,0},{9,1},... | collective-permute-start | bytes 196616 | tf_op jit(solution)/shard_map/ppermute | solution.py:953
  229.6 17.2 %collective-permute-start.20 = (bf16[1,1024,128]{2,1,0:T(8,128)(2,1)S(1)}, bf16[1,1024,128]{2,1,0:T(8,128)(2,1)S(1)}, u32[]{:S(2)}, u32[]{:S(2)}) collective-permute-start(bf16[1,1024,128]{2,1,0:T(8,128)(2,1)S(1)} %add_convert_fusion.9), channel_id=1, source_target_pairs={{0,16},{1,17},{2,18},{3,19},{4,20},{5,21},{6,22},{7,23},{8,24},{9,... | collective-permute-start | bytes 786440 | tf_op jit(solution)/shard_map/ppermute | solution.py:953
  232.4 14.4 %collective-permute-start.21 = (f32[32,512]{1,0:T(8,128)S(1)}, f32[32,512]{1,0:T(8,128)S(1)}, u32[]{:S(2)}, u32[]{:S(2)}) collective-permute-start(f32[32,512]{1,0:T(8,128)S(1)} %add.141), channel_id=1, source_target_pairs={{0,16},{1,17},{2,18},{3,19},{4,20},{5,21},{6,22},{7,23},{8,24},{9,... | collective-permute-start | bytes 196616 | tf_op jit(solution)/shard_map/ppermute | solution.py:953
  246.9 7.5 %collective-permute-start.26 = (bf16[1024,128]{1,0:T(8,128)(2,1)S(1)}, bf16[1024,128]{1,0:T(8,128)(2,1)S(1)}, u32[]{:S(2)}, u32[]{:S(2)}) collective-permute-start(bf16[1024,128]{1,0:T(8,128)(2,1)S(1)} %get-tuple-element.166), channel_id=1, source_target_pairs={{0,2},{1,3},{4,6},{5,7},{8,10},{9,11},{12,14},{13,15},{16,18},{17,... | collective-permute-start | bytes 786440 | tf_op jit(solution)/shard_map/ppermute | solution.py:953
  249.3 5.1 %collective-permute-start.22 = (f32[32,512]{1,0:T(8,128)S(1)}, f32[32,512]{1,0:T(8,128)S(1)}, u32[]{:S(2)}, u32[]{:S(2)}) collective-permute-start(f32[32,512]{1,0:T(8,128)S(1)} %add.146), channel_id=1, source_target_pairs={{0,4},{1,5},{2,6},{3,7},{4,0},{5,1},{6,2},{7,3},{8,12},{9,13},{10,... | collective-permute-start | bytes 196616 | tf_op jit(solution)/shard_map/ppermute | solution.py:953
  264.9 25.6 %collective-permute-start.31 = (bf16[512,128]{1,0:T(8,128)(2,1)S(1)}, bf16[512,128]{1,0:T(8,128)(2,1)S(1)}, u32[]{:S(2)}, u32[]{:S(2)}) collective-permute-start(bf16[512,128]{1,0:T(8,128)(2,1)S(1)} %pad_maximum_fusion.1), channel_id=1, source_target_pairs={{1,0},{5,4},{9,8},{13,12},{17,16},{21,20},{25,24},{29,28}} | collective-permute-start | bytes 393224 | tf_op jit(solution)/shard_map/ppermute | solution.py:953
  (42 other events, 666.8 us)
